TPU v7x, 256 devices: a whole 4x4x8 slice. The times are simulated.
256 devices in a mesh: row: 32 (over z, x), col: 8 (over y, core).
Axes of the slice: x: 4, y: 4, z: 8, core: 2. Of those that a mesh axis runs over, the one named last changes fastest.
Arguments:
- moving_slab: float32 [32, 512, 1024], P('row', None, 'col'), may hold values from -6 to 6
- fixed_image: float32 [32, 512, 1024], P(None, 'row', 'col'), may hold values from -6 to 6
- start_field: float32 [3, 32, 512, 1024], P(None, None, 'row', 'col'), may hold values from -6 to 6
- tissue_mask: int32 [4, 32, 8], replicated, may hold values 0 or 1
Outputs:
- displacement: float32 [3, 32, 512, 1024], P(None, None, 'row', 'col')
All inputs are finite; a program needn't handle non-finite values.
Results may differ from a plain program's by a relative error of at most 0.000084.
Values sent between devices are 32-bit elements; how exact they have to be, the bound alone decides.
No kernel may reach another device: no remote copies, remote signals or barrier semaphores. Data moves between devices by JAX's collectives and lax.ppermute only.
A program may use at most 64 MiB of HBM per device.

v0:
```python
import jax
import jax.numpy as jnp
from jax import lax
from jax.sharding import PartitionSpec as P

ITERS = 3


pull_rate = 1.0
smooth_rate = 0.16


def with_halo(x, sides, width):
    for axis, dim in sides:
        size, length = (lax.axis_size(axis), x.shape[dim])
        up = [(i, (i + 1) % size) for i in range(size - 1)]
        down = [(j, i) for i, j in up]
        last = lax.slice_in_dim(x, length - width, length, axis=dim)
        initial = lax.slice_in_dim(x, 0, width, axis=dim)
        before = lax.ppermute(last, axis, up)
        after = lax.ppermute(initial, axis, down)
        x = jnp.concatenate([before, x, after], axis=dim)
    return x


def gradient(extended):
    padded = jnp.pad(extended[:, 1:-1, 1:-1], ((1, 1), (0, 0), (0, 0)))
    grad_z = 0.5 * (padded[2:] - padded[:-2])
    grad_y = 0.5 * (extended[:, 2:, 1:-1] - extended[:, :-2, 1:-1])
    grad_x = 0.5 * (extended[:, 1:-1, 2:] - extended[:, 1:-1, :-2])
    return jnp.stack([grad_z, grad_y, grad_x])


def attract(displace, slopes, fixed, moving, tissue):
    residual = (
        fixed
        - moving
        - (slopes[0] * displace[0] + slopes[1] * displace[1] + slopes[2] * displace[2])
    )
    denominator = (
        slopes[0] * slopes[0]
        + slopes[1] * slopes[1]
        + slopes[2] * slopes[2]
        + residual * residual
        + 0.5
    )
    return tissue * (displace + pull_rate * residual * slopes / denominator)


def window(array, shift_z, shift_y, shift_x):
    extent_z, extent_y, extent_x = array.shape[-3:]
    return array[
        ...,
        1 + shift_z : extent_z - 1 + shift_z,
        1 + shift_y : extent_y - 1 + shift_y,
        1 + shift_x : extent_x - 1 + shift_x,
    ]


def smooth(extended, tissue_rim):
    field_pad = jnp.pad(extended, ((0, 0), (1, 1), (0, 0), (0, 0)))
    tissue_pad = jnp.pad(tissue_rim, ((1, 1), (0, 0), (0, 0)))
    centre = window(field_pad, 0, 0, 0)
    centre_tissue = window(tissue_pad, 0, 0, 0)
    flow = jnp.zeros_like(centre)
    for offset in ((1, 0, 0), (-1, 0, 0), (0, 1, 0), (0, -1, 0), (0, 0, 1), (0, 0, -1)):
        flow = flow + window(tissue_pad, *offset) * (window(field_pad, *offset) - centre)
    return centre + smooth_rate * centre_tissue * flow


def tissue_cells(
    tissue_mask, z_extent, row_start, col_start, row_count, col_count, brick_rows, brick_cols
):
    table = tissue_mask.astype(jnp.float32)
    count_z, count_y, count_x = table.shape
    row_ids = row_start + jnp.arange(row_count, dtype=jnp.int32)
    col_ids = col_start + jnp.arange(col_count, dtype=jnp.int32)
    pick_rows = (
        (row_ids // brick_rows)[None, :] == jnp.arange(count_y, dtype=jnp.int32)[:, None]
    ).astype(jnp.float32)
    pick_cols = (
        (col_ids // brick_cols)[None, :] == jnp.arange(count_x, dtype=jnp.int32)[:, None]
    ).astype(jnp.float32)
    blocks = jnp.einsum(
        "kab,ay,bw->kyw", table, pick_rows, pick_cols, precision=lax.Precision.HIGHEST
    )
    return jnp.repeat(blocks, z_extent // count_z, axis=0)


def trimmed(array):
    return array[..., 1:-1, 1:-1]


def body(moving_slab, fixed_image, start_field, tissue_mask):
    moving = lax.all_to_all(moving_slab, "row", split_axis=1, concat_axis=0, tiled=True)
    z_extent, brick_rows, brick_cols = moving.shape
    row_index = lax.axis_index("row")
    col_index = lax.axis_index("col")
    moving_rim = with_halo(moving, (("row", 1), ("col", 2)), 1)
    slopes = gradient(moving_rim)
    tissue_rim = tissue_cells(
        tissue_mask,
        z_extent,
        row_index * brick_rows - 1,
        col_index * brick_cols - 1,
        brick_rows + 2,
        brick_cols + 2,
        brick_rows,
        brick_cols,
    )
    tissue = trimmed(tissue_rim)
    displace = start_field
    for sweep in range(ITERS):
        pulled = attract(displace, slopes, fixed_image, moving, tissue)
        pulled_rim = with_halo(pulled, (("row", 2), ("col", 3)), 1)
        displace = smooth(pulled_rim, tissue_rim)
    return displace


def solution(mesh):
    in_specs = (P("row", None, "col"), P(None, "row", "col"), P(None, None, "row", "col"), P())
    out_specs = P(None, None, "row", "col")
    return jax.shard_map(body, mesh=mesh, in_specs=in_specs, out_specs=out_specs, check_vma=False)
```

profile of v0, /device:TPU:126, one launch (start us, length us, event | category | flops | bytes accessed | tf_op | source)
XLA Modules:
  0.0 116.8 jit_solution(10778929158189394029)
XLA Ops:
  0.0 10.2 %all-to-all-start = ((f32[1,512,128]{2,0,1:T(1,128)}), f32[1,512,128]{2,0,1:T(1,128)S(1)}, u32[]{:S(2)}, u32[]{:S(2)}) async-start(f32[1,512,128]{2,0,1:T(1,128)} %bitcast.107), calls=%async_computation | async-start | bytes 524288 | tf_op jit(solution)/shard_map/all_to_all | solution.py:95
  10.2 0.9 convolution_bitcast_fusion.1
  11.5 8.0 %all-to-all-done = f32[1,512,128]{2,0,1:T(1,128)S(1)} async-done(((f32[1,512,128]{2,0,1:T(1,128)}), f32[1,512,128]{2,0,1:T(1,128)S(1)}, u32[]{:S(2)}, u32[]{:S(2)}) %all-to-all-start) | async-done | bytes 262176 | tf_op jit(solution)/shard_map/all_to_all | solution.py:95
  19.5 3.9 %collective-permute-start.1 = (f32[32,1,128]{2,0,1:T(8,128)S(1)}, f32[32,1,128]{2,0,1:T(8,128)S(1)}, u32[]{:S(2)}, u32[]{:S(2)}) collective-permute-start(f32[32,1,128]{2,0,1:T(8,128)S(1)} %get-tuple-element.38), channel_id=1, source_target_pairs={{0,8},{8,16},{16,24},{24,32},{32,40},{40,48},{48,56},{56,64},{64,7... | collective-permute-start | bytes 49160 | tf_op jit(solution)/shard_map/ppermute | solution.py:20
  23.5 1.9 %collective-permute-start = (f32[32,1,128]{2,0,1:T(8,128)S(1)}, f32[32,1,128]{2,0,1:T(8,128)S(1)}, u32[]{:S(2)}, u32[]{:S(2)}) collective-permute-start(f32[32,1,128]{2,0,1:T(8,128)S(1)} %get-tuple-element.37), channel_id=1, source_target_pairs={{8,0},{16,8},{24,16},{32,24},{40,32},{48,40},{56,48},{64,56},{72,6... | collective-permute-start | bytes 49160 | tf_op jit(solution)/shard_map/ppermute | solution.py:21
  25.6 6.9 %collective-permute-done = f32[32,1,128]{2,0,1:T(8,128)S(1)} collective-permute-done((f32[32,1,128]{2,0,1:T(8,128)S(1)}, f32[32,1,128]{2,0,1:T(8,128)S(1)}, u32[]{:S(2)}, u32[]{:S(2)}) %collective-permute-start) | collective-permute-done | bytes 16416 | tf_op jit(solution)/shard_map/ppermute | solution.py:21
  32.6 2.1 %collective-permute-start.2 = (f32[32,18,1]{2,0,1:T(8,128)S(1)}, f32[32,18,1]{2,0,1:T(8,128)S(1)}, u32[]{:S(2)}, u32[]{:S(2)}) collective-permute-start(f32[32,18,1]{2,0,1:T(8,128)S(1)} %get-tuple-element.35), channel_id=1, source_target_pairs={{1,0},{2,1},{3,2},{4,3},{5,4},{6,5},{7,6},{9,8},{10,9},{11,10},{12... | collective-permute-start | bytes 6920 | tf_op jit(solution)/shard_map/ppermute | solution.py:21
  34.7 2.6 %collective-permute-start.3 = (f32[32,18,1]{2,0,1:T(8,128)S(1)}, f32[32,18,1]{2,0,1:T(8,128)S(1)}, u32[]{:S(2)}, u32[]{:S(2)}) collective-permute-start(f32[32,18,1]{2,0,1:T(8,128)S(1)} %get-tuple-element.36), channel_id=1, source_target_pairs={{0,1},{1,2},{2,3},{3,4},{4,5},{5,6},{6,7},{8,9},{9,10},{10,11},{11... | collective-permute-start | bytes 6920 | tf_op jit(solution)/shard_map/ppermute | solution.py:20
  37.3 1.7 %broadcast_multiply_fusion = (f32[32,16,128]{2,0,1:T(8,128)}, f32[32,16,128]{2,0,1:T(8,128)}, f32[32,16,128]{2,0,1:T(8,128)}, f32[32,16,128]{2,0,1:T(8,128)}, f3...) fusion(f32[32,18,130]{2,0,1:T(8,128)S(1)} %broadcast_bitcast_fusion), kind=kLoop, calls=%fused_computation.152 | loop fusion | flops 65536 | bytes 3997696 | tf_op jit(solution)/shard_map/mul | solution.py:68
  39.2 3.6 %collective-permute-done.3 = f32[32,18,1]{2,0,1:T(8,128)S(1)} collective-permute-done((f32[32,18,1]{2,0,1:T(8,128)S(1)}, f32[32,18,1]{2,0,1:T(8,128)S(1)}, u32[]{:S(2)}, u32[]{:S(2)}) %collective-permute-start.3) | collective-permute-done | bytes 2336 | tf_op jit(solution)/shard_map/ppermute | solution.py:20
  42.9 1.1 add_add_fusion.2
  44.4 1.9 %collective-permute-start.4 = (f32[3,32,1,128]{3,1,2,0:T(8,128)S(1)}, f32[3,32,1,128]{3,1,2,0:T(8,128)S(1)}, u32[]{:S(2)}, u32[]{:S(2)}) collective-permute-start(f32[3,32,1,128]{3,1,2,0:T(8,128)S(1)} %get-tuple-element.24), channel_id=1, source_target_pairs={{0,8},{8,16},{16,24},{24,32},{32,40},{40,48},{48,56},{56,64},{64,7... | collective-permute-start | bytes 147464 | tf_op jit(solution)/shard_map/ppermute | solution.py:20
  46.3 3.9 %collective-permute-start.5 = (f32[3,32,1,128]{3,1,2,0:T(8,128)S(1)}, f32[3,32,1,128]{3,1,2,0:T(8,128)S(1)}, u32[]{:S(2)}, u32[]{:S(2)}) collective-permute-start(f32[3,32,1,128]{3,1,2,0:T(8,128)S(1)} %get-tuple-element.25), channel_id=1, source_target_pairs={{8,0},{16,8},{24,16},{32,24},{40,32},{48,40},{56,48},{64,56},{72,6... | collective-permute-start | bytes 147464 | tf_op jit(solution)/shard_map/ppermute | solution.py:21
  50.4 5.2 %collective-permute-done.5 = f32[3,32,1,128]{3,1,2,0:T(8,128)S(1)} collective-permute-done((f32[3,32,1,128]{3,1,2,0:T(8,128)S(1)}, f32[3,32,1,128]{3,1,2,0:T(8,128)S(1)}, u32[]{:S(2)}, u32[]{:S(2)}) %collective-permute-start.5) | collective-permute-done | bytes 49184 | tf_op jit(solution)/shard_map/ppermute | solution.py:21
  56.0 0.5 copy.116
  56.5 1.9 %collective-permute-start.7 = (f32[3,32,18,1]{1,2,3,0:T(8,128)S(1)}, f32[3,32,18,1]{1,2,3,0:T(8,128)S(1)}, u32[]{:S(2)}, u32[]{:S(2)}) collective-permute-start(f32[3,32,18,1]{1,2,3,0:T(8,128)S(1)} %copy.116), channel_id=1, source_target_pairs={{1,0},{2,1},{3,2},{4,3},{5,4},{6,5},{7,6},{9,8},{10,9},{11,10},{12... | collective-permute-start | bytes 20744 | tf_op jit(solution)/shard_map/ppermute | solution.py:21
  58.4 0.5 copy.115
  58.9 2.4 %collective-permute-start.6 = (f32[3,32,18,1]{1,2,3,0:T(8,128)S(1)}, f32[3,32,18,1]{1,2,3,0:T(8,128)S(1)}, u32[]{:S(2)}, u32[]{:S(2)}) collective-permute-start(f32[3,32,18,1]{1,2,3,0:T(8,128)S(1)} %copy.115), channel_id=1, source_target_pairs={{0,1},{1,2},{2,3},{3,4},{4,5},{5,6},{6,7},{8,9},{9,10},{10,11},{11... | collective-permute-start | bytes 20744 | tf_op jit(solution)/shard_map/ppermute | solution.py:20
  61.3 0.4 copy.99
  61.7 2.5 %collective-permute-done.6 = f32[3,32,18,1]{1,2,3,0:T(8,128)S(1)} collective-permute-done((f32[3,32,18,1]{1,2,3,0:T(8,128)S(1)}, f32[3,32,18,1]{1,2,3,0:T(8,128)S(1)}, u32[]{:S(2)}, u32[]{:S(2)}) %collective-permute-start.6) | collective-permute-done | bytes 6944 | tf_op jit(solution)/shard_map/ppermute | solution.py:20
  64.2 0.4 copy.98
  64.7 1.0 select_maximum_fusion.8
  66.0 1.1 fusion.39
  67.6 0.5 copy-done.4
  68.5 1.9 %collective-permute-start.8 = (f32[3,32,1,128]{3,1,2,0:T(8,128)S(1)}, f32[3,32,1,128]{3,1,2,0:T(8,128)S(1)}, u32[]{:S(2)}, u32[]{:S(2)}) collective-permute-start(f32[3,32,1,128]{3,1,2,0:T(8,128)S(1)} %get-tuple-element.22), channel_id=1, source_target_pairs={{0,8},{8,16},{16,24},{24,32},{32,40},{40,48},{48,56},{56,64},{64,7... | collective-permute-start | bytes 147464 | tf_op jit(solution)/shard_map/ppermute | solution.py:20
  70.4 3.9 %collective-permute-start.9 = (f32[3,32,1,128]{3,1,2,0:T(8,128)S(1)}, f32[3,32,1,128]{3,1,2,0:T(8,128)S(1)}, u32[]{:S(2)}, u32[]{:S(2)}) collective-permute-start(f32[3,32,1,128]{3,1,2,0:T(8,128)S(1)} %get-tuple-element.23), channel_id=1, source_target_pairs={{8,0},{16,8},{24,16},{32,24},{40,32},{48,40},{56,48},{64,56},{72,6... | collective-permute-start | bytes 147464 | tf_op jit(solution)/shard_map/ppermute | solution.py:21
  74.5 5.2 %collective-permute-done.9 = f32[3,32,1,128]{3,1,2,0:T(8,128)S(1)} collective-permute-done((f32[3,32,1,128]{3,1,2,0:T(8,128)S(1)}, f32[3,32,1,128]{3,1,2,0:T(8,128)S(1)}, u32[]{:S(2)}, u32[]{:S(2)}) %collective-permute-start.9) | collective-permute-done | bytes 49184 | tf_op jit(solution)/shard_map/ppermute | solution.py:21
  80.1 0.5 copy.118
  80.6 1.9 %collective-permute-start.11 = (f32[3,32,18,1]{1,2,3,0:T(8,128)S(1)}, f32[3,32,18,1]{1,2,3,0:T(8,128)S(1)}, u32[]{:S(2)}, u32[]{:S(2)}) collective-permute-start(f32[3,32,18,1]{1,2,3,0:T(8,128)S(1)} %copy.118), channel_id=1, source_target_pairs={{1,0},{2,1},{3,2},{4,3},{5,4},{6,5},{7,6},{9,8},{10,9},{11,10},{12... | collective-permute-start | bytes 20744 | tf_op jit(solution)/shard_map/ppermute | solution.py:21
  82.6 0.5 copy.117
  83.0 2.4 %collective-permute-start.10 = (f32[3,32,18,1]{1,2,3,0:T(8,128)S(1)}, f32[3,32,18,1]{1,2,3,0:T(8,128)S(1)}, u32[]{:S(2)}, u32[]{:S(2)}) collective-permute-start(f32[3,32,18,1]{1,2,3,0:T(8,128)S(1)} %copy.117), channel_id=1, source_target_pairs={{0,1},{1,2},{2,3},{3,4},{4,5},{5,6},{6,7},{8,9},{9,10},{10,11},{11... | collective-permute-start | bytes 20744 | tf_op jit(solution)/shard_map/ppermute | solution.py:20
  85.5 0.4 copy.105
  85.9 2.5 %collective-permute-done.10 = f32[3,32,18,1]{1,2,3,0:T(8,128)S(1)} collective-permute-done((f32[3,32,18,1]{1,2,3,0:T(8,128)S(1)}, f32[3,32,18,1]{1,2,3,0:T(8,128)S(1)}, u32[]{:S(2)}, u32[]{:S(2)}) %collective-permute-start.10) | collective-permute-done | bytes 6944 | tf_op jit(solution)/shard_map/ppermute | solution.py:20
  88.8 1.0 select_maximum_fusion.4
  90.2 1.1 fusion.22
  91.7 0.5 copy-done.5
  92.7 1.9 %collective-permute-start.12 = (f32[3,32,1,128]{3,1,2,0:T(8,128)S(1)}, f32[3,32,1,128]{3,1,2,0:T(8,128)S(1)}, u32[]{:S(2)}, u32[]{:S(2)}) collective-permute-start(f32[3,32,1,128]{3,1,2,0:T(8,128)S(1)} %get-tuple-element.20), channel_id=1, source_target_pairs={{0,8},{8,16},{16,24},{24,32},{32,40},{40,48},{48,56},{56,64},{64,7... | collective-permute-start | bytes 147464 | tf_op jit(solution)/shard_map/ppermute | solution.py:20
  94.6 4.1 %collective-permute-start.13 = (f32[3,32,1,128]{3,1,2,0:T(8,128)S(1)}, f32[3,32,1,128]{3,1,2,0:T(8,128)S(1)}, u32[]{:S(2)}, u32[]{:S(2)}) collective-permute-start(f32[3,32,1,128]{3,1,2,0:T(8,128)S(1)} %get-tuple-element.21), channel_id=1, source_target_pairs={{8,0},{16,8},{24,16},{32,24},{40,32},{48,40},{56,48},{64,56},{72,6... | collective-permute-start | bytes 147464 | tf_op jit(solution)/shard_map/ppermute | solution.py:21
  98.7 5.2 %collective-permute-done.13 = f32[3,32,1,128]{3,1,2,0:T(8,128)S(1)} collective-permute-done((f32[3,32,1,128]{3,1,2,0:T(8,128)S(1)}, f32[3,32,1,128]{3,1,2,0:T(8,128)S(1)}, u32[]{:S(2)}, u32[]{:S(2)}) %collective-permute-start.13) | collective-permute-done | bytes 49184 | tf_op jit(solution)/shard_map/ppermute | solution.py:21
  104.3 0.5 copy.120
  104.8 1.9 %collective-permute-start.15 = (f32[3,32,18,1]{1,2,3,0:T(8,128)S(1)}, f32[3,32,18,1]{1,2,3,0:T(8,128)S(1)}, u32[]{:S(2)}, u32[]{:S(2)}) collective-permute-start(f32[3,32,18,1]{1,2,3,0:T(8,128)S(1)} %copy.120), channel_id=1, source_target_pairs={{1,0},{2,1},{3,2},{4,3},{5,4},{6,5},{7,6},{9,8},{10,9},{11,10},{12... | collective-permute-start | bytes 20744 | tf_op jit(solution)/shard_map/ppermute | solution.py:21
  106.7 0.5 copy.119
  107.2 2.4 %collective-permute-start.14 = (f32[3,32,18,1]{1,2,3,0:T(8,128)S(1)}, f32[3,32,18,1]{1,2,3,0:T(8,128)S(1)}, u32[]{:S(2)}, u32[]{:S(2)}) collective-permute-start(f32[3,32,18,1]{1,2,3,0:T(8,128)S(1)} %copy.119), channel_id=1, source_target_pairs={{0,1},{1,2},{2,3},{3,4},{4,5},{5,6},{6,7},{8,9},{9,10},{10,11},{11... | collective-permute-start | bytes 20744 | tf_op jit(solution)/shard_map/ppermute | solution.py:20
  109.6 0.4 copy.111
  110.0 2.5 %collective-permute-done.14 = f32[3,32,18,1]{1,2,3,0:T(8,128)S(1)} collective-permute-done((f32[3,32,18,1]{1,2,3,0:T(8,128)S(1)}, f32[3,32,18,1]{1,2,3,0:T(8,128)S(1)}, u32[]{:S(2)}, u32[]{:S(2)}) %collective-permute-start.14) | collective-permute-done | bytes 6944 | tf_op jit(solution)/shard_map/ppermute | solution.py:20
  112.9 1.0 select_maximum_fusion
  114.3 1.1 fusion.5
  115.5 1.3 %copy.114 = f32[3,32,16,128]{3,2,1,0:T(8,128)} copy(f32[3,32,16,128]{3,1,2,0:T(8,128)S(1)} %fusion.5) | data formatting | bytes 1572864 | tf_op jit(solution)/shard_map/add | solution.py:68
  (106 shorter events, 6.2 us)
Async XLA Ops:
  0.0 19.4 %all-to-all-start = ((f32[1,512,128]{2,0,1:T(1,128)}), f32[1,512,128]{2,0,1:T(1,128)S(1)}, u32[]{:S(2)}, u32[]{:S(2)}) async-start(f32[1,512,128]{2,0,1:T(1,128)} %bitcast.107), calls=%async_computation | async-start | bytes 524288 | tf_op jit(solution)/shard_map/all_to_all | solution.py:95
  19.5 23.4 %copy-start = (f32[32,16,128]{2,0,1:T(8,128)}, f32[32,16,128]{2,0,1:T(8,128)S(1)}, u32[]{:S(2)}) copy-start(f32[32,16,128]{2,0,1:T(8,128)S(1)} %copy.85) | copy-start | bytes 786436
  19.5 5.9 %collective-permute-start.1 = (f32[32,1,128]{2,0,1:T(8,128)S(1)}, f32[32,1,128]{2,0,1:T(8,128)S(1)}, u32[]{:S(2)}, u32[]{:S(2)}) collective-permute-start(f32[32,1,128]{2,0,1:T(8,128)S(1)} %get-tuple-element.38), channel_id=1, source_target_pairs={{0,8},{8,16},{16,24},{24,32},{32,40},{40,48},{48,56},{56,64},{64,7... | collective-permute-start | bytes 49160 | tf_op jit(solution)/shard_map/ppermute | solution.py:20
  23.5 9.0 %collective-permute-start = (f32[32,1,128]{2,0,1:T(8,128)S(1)}, f32[32,1,128]{2,0,1:T(8,128)S(1)}, u32[]{:S(2)}, u32[]{:S(2)}) collective-permute-start(f32[32,1,128]{2,0,1:T(8,128)S(1)} %get-tuple-element.37), channel_id=1, source_target_pairs={{8,0},{16,8},{24,16},{32,24},{40,32},{48,40},{56,48},{64,56},{72,6... | collective-permute-start | bytes 49160 | tf_op jit(solution)/shard_map/ppermute | solution.py:21
  32.6 6.3 %copy-start.30 = (f32[3,32,16,128]{3,2,1,0:T(8,128)S(1)}, f32[3,32,16,128]{3,2,1,0:T(8,128)}, u32[]{:S(2)}) copy-start(f32[3,32,16,128]{3,2,1,0:T(8,128)} %param.6) | copy-start | bytes 2359300
  32.6 6.6 %collective-permute-start.2 = (f32[32,18,1]{2,0,1:T(8,128)S(1)}, f32[32,18,1]{2,0,1:T(8,128)S(1)}, u32[]{:S(2)}, u32[]{:S(2)}) collective-permute-start(f32[32,18,1]{2,0,1:T(8,128)S(1)} %get-tuple-element.35), channel_id=1, source_target_pairs={{1,0},{2,1},{3,2},{4,3},{5,4},{6,5},{7,6},{9,8},{10,9},{11,10},{12... | collective-permute-start | bytes 6920 | tf_op jit(solution)/shard_map/ppermute | solution.py:21
  34.7 8.2 %copy-start.31 = (f32[32,16,128]{2,1,0:T(8,128)S(1)}, f32[32,16,128]{2,1,0:T(8,128)}, u32[]{:S(2)}) copy-start(f32[32,16,128]{2,1,0:T(8,128)} %param.5) | copy-start | bytes 786436
  34.7 8.2 %collective-permute-start.3 = (f32[32,18,1]{2,0,1:T(8,128)S(1)}, f32[32,18,1]{2,0,1:T(8,128)S(1)}, u32[]{:S(2)}, u32[]{:S(2)}) collective-permute-start(f32[32,18,1]{2,0,1:T(8,128)S(1)} %get-tuple-element.36), channel_id=1, source_target_pairs={{0,1},{1,2},{2,3},{3,4},{4,5},{5,6},{6,7},{8,9},{9,10},{10,11},{11... | collective-permute-start | bytes 6920 | tf_op jit(solution)/shard_map/ppermute | solution.py:20
  39.0 5.0 %copy-start.6 = (f32[32,16,128]{2,0,1:T(8,128)}, f32[32,16,128]{2,0,1:T(8,128)S(1)}, u32[]{:S(2)}) copy-start(f32[32,16,128]{2,0,1:T(8,128)S(1)} %get-tuple-element.33) | copy-start | bytes 786436
  44.0 11.7 %copy-start.3 = (f32[1,32,16,128]{3,1,2,0:T(8,128)}, f32[1,32,16,128]{3,1,2,0:T(8,128)S(1)}, u32[]{:S(2)}) copy-start(f32[1,32,16,128]{3,1,2,0:T(8,128)S(1)} %get-tuple-element.34) | copy-start | bytes 786436
  44.4 6.0 %collective-permute-start.4 = (f32[3,32,1,128]{3,1,2,0:T(8,128)S(1)}, f32[3,32,1,128]{3,1,2,0:T(8,128)S(1)}, u32[]{:S(2)}, u32[]{:S(2)}) collective-permute-start(f32[3,32,1,128]{3,1,2,0:T(8,128)S(1)} %get-tuple-element.24), channel_id=1, source_target_pairs={{0,8},{8,16},{16,24},{24,32},{32,40},{40,48},{48,56},{56,64},{64,7... | collective-permute-start | bytes 147464 | tf_op jit(solution)/shard_map/ppermute | solution.py:20
  46.3 9.3 %collective-permute-start.5 = (f32[3,32,1,128]{3,1,2,0:T(8,128)S(1)}, f32[3,32,1,128]{3,1,2,0:T(8,128)S(1)}, u32[]{:S(2)}, u32[]{:S(2)}) collective-permute-start(f32[3,32,1,128]{3,1,2,0:T(8,128)S(1)} %get-tuple-element.25), channel_id=1, source_target_pairs={{8,0},{16,8},{24,16},{32,24},{40,32},{48,40},{56,48},{64,56},{72,6... | collective-permute-start | bytes 147464 | tf_op jit(solution)/shard_map/ppermute | solution.py:21
  56.5 4.8 %collective-permute-start.7 = (f32[3,32,18,1]{1,2,3,0:T(8,128)S(1)}, f32[3,32,18,1]{1,2,3,0:T(8,128)S(1)}, u32[]{:S(2)}, u32[]{:S(2)}) collective-permute-start(f32[3,32,18,1]{1,2,3,0:T(8,128)S(1)} %copy.116), channel_id=1, source_target_pairs={{1,0},{2,1},{3,2},{4,3},{5,4},{6,5},{7,6},{9,8},{10,9},{11,10},{12... | collective-permute-start | bytes 20744 | tf_op jit(solution)/shard_map/ppermute | solution.py:21
  58.9 5.3 %collective-permute-start.6 = (f32[3,32,18,1]{1,2,3,0:T(8,128)S(1)}, f32[3,32,18,1]{1,2,3,0:T(8,128)S(1)}, u32[]{:S(2)}, u32[]{:S(2)}) collective-permute-start(f32[3,32,18,1]{1,2,3,0:T(8,128)S(1)} %copy.115), channel_id=1, source_target_pairs={{0,1},{1,2},{2,3},{3,4},{4,5},{5,6},{6,7},{8,9},{9,10},{10,11},{11... | collective-permute-start | bytes 20744 | tf_op jit(solution)/shard_map/ppermute | solution.py:20
  64.6 1.0 copy-start.9
  64.6 1.0 copy-start.12
  64.6 1.1 copy-start.15
  64.6 1.2 copy-start.18
  64.6 1.2 %copy-start.21 = (f32[32,16,128]{2,0,1:T(8,128)S(1)}, f32[32,16,128]{2,0,1:T(8,128)}, u32[]{:S(2)}) copy-start(f32[32,16,128]{2,0,1:T(8,128)} %get-tuple-element.30) | copy-start | bytes 786436
  64.6 1.3 %copy-start.24 = (f32[32,16,128]{2,0,1:T(8,128)S(1)}, f32[32,16,128]{2,0,1:T(8,128)}, u32[]{:S(2)}) copy-start(f32[32,16,128]{2,0,1:T(8,128)} %get-tuple-element.31) | copy-start | bytes 786436
  64.7 1.4 %copy-start.27 = (f32[32,16,128]{2,0,1:T(8,128)S(1)}, f32[32,16,128]{2,0,1:T(8,128)}, u32[]{:S(2)}) copy-start(f32[32,16,128]{2,0,1:T(8,128)} %get-tuple-element.32) | copy-start | bytes 786436
  66.0 1.2 %copy-start.1 = (f32[32,16,128]{2,0,1:T(8,128)S(1)}, f32[32,16,128]{2,0,1:T(8,128)}, u32[]{:S(2)}) copy-start(f32[32,16,128]{2,0,1:T(8,128)} %copy-done) | copy-start | bytes 786436
  66.0 1.2 %copy-start.32 = (f32[32,16,128]{2,1,0:T(8,128)S(1)}, f32[32,16,128]{2,1,0:T(8,128)}, u32[]{:S(2)}) copy-start(f32[32,16,128]{2,1,0:T(8,128)} %param.5) | copy-start | bytes 786436
  66.0 1.2 %copy-start.34 = (f32[32,16,128]{2,0,1:T(8,128)S(1)}, f32[32,16,128]{2,0,1:T(8,128)}, u32[]{:S(2)}) copy-start(f32[32,16,128]{2,0,1:T(8,128)} %get-tuple-element.11) | copy-start | bytes 786436
  68.5 6.0 %collective-permute-start.8 = (f32[3,32,1,128]{3,1,2,0:T(8,128)S(1)}, f32[3,32,1,128]{3,1,2,0:T(8,128)S(1)}, u32[]{:S(2)}, u32[]{:S(2)}) collective-permute-start(f32[3,32,1,128]{3,1,2,0:T(8,128)S(1)} %get-tuple-element.22), channel_id=1, source_target_pairs={{0,8},{8,16},{16,24},{24,32},{32,40},{40,48},{48,56},{56,64},{64,7... | collective-permute-start | bytes 147464 | tf_op jit(solution)/shard_map/ppermute | solution.py:20
  70.4 9.3 %collective-permute-start.9 = (f32[3,32,1,128]{3,1,2,0:T(8,128)S(1)}, f32[3,32,1,128]{3,1,2,0:T(8,128)S(1)}, u32[]{:S(2)}, u32[]{:S(2)}) collective-permute-start(f32[3,32,1,128]{3,1,2,0:T(8,128)S(1)} %get-tuple-element.23), channel_id=1, source_target_pairs={{8,0},{16,8},{24,16},{32,24},{40,32},{48,40},{56,48},{64,56},{72,6... | collective-permute-start | bytes 147464 | tf_op jit(solution)/shard_map/ppermute | solution.py:21
  80.6 4.8 %collective-permute-start.11 = (f32[3,32,18,1]{1,2,3,0:T(8,128)S(1)}, f32[3,32,18,1]{1,2,3,0:T(8,128)S(1)}, u32[]{:S(2)}, u32[]{:S(2)}) collective-permute-start(f32[3,32,18,1]{1,2,3,0:T(8,128)S(1)} %copy.118), channel_id=1, source_target_pairs={{1,0},{2,1},{3,2},{4,3},{5,4},{6,5},{7,6},{9,8},{10,9},{11,10},{12... | collective-permute-start | bytes 20744 | tf_op jit(solution)/shard_map/ppermute | solution.py:21
  83.0 5.3 %collective-permute-start.10 = (f32[3,32,18,1]{1,2,3,0:T(8,128)S(1)}, f32[3,32,18,1]{1,2,3,0:T(8,128)S(1)}, u32[]{:S(2)}, u32[]{:S(2)}) collective-permute-start(f32[3,32,18,1]{1,2,3,0:T(8,128)S(1)} %copy.117), channel_id=1, source_target_pairs={{0,1},{1,2},{2,3},{3,4},{4,5},{5,6},{6,7},{8,9},{9,10},{10,11},{11... | collective-permute-start | bytes 20744 | tf_op jit(solution)/shard_map/ppermute | solution.py:20
  88.7 1.0 copy-start.10
  88.7 1.0 copy-start.13
  88.7 1.1 copy-start.16
  88.7 1.2 copy-start.19
  88.8 1.2 %copy-start.22 = (f32[32,16,128]{2,0,1:T(8,128)S(1)}, f32[32,16,128]{2,0,1:T(8,128)}, u32[]{:S(2)}) copy-start(f32[32,16,128]{2,0,1:T(8,128)} %get-tuple-element.30) | copy-start | bytes 786436
  88.8 1.3 %copy-start.25 = (f32[32,16,128]{2,0,1:T(8,128)S(1)}, f32[32,16,128]{2,0,1:T(8,128)}, u32[]{:S(2)}) copy-start(f32[32,16,128]{2,0,1:T(8,128)} %get-tuple-element.31) | copy-start | bytes 786436
  88.8 1.4 %copy-start.28 = (f32[32,16,128]{2,0,1:T(8,128)S(1)}, f32[32,16,128]{2,0,1:T(8,128)}, u32[]{:S(2)}) copy-start(f32[32,16,128]{2,0,1:T(8,128)} %get-tuple-element.32) | copy-start | bytes 786436
  90.2 1.2 copy-start.2
  90.2 1.2 %copy-start.33 = (f32[32,16,128]{2,1,0:T(8,128)S(1)}, f32[32,16,128]{2,1,0:T(8,128)}, u32[]{:S(2)}) copy-start(f32[32,16,128]{2,1,0:T(8,128)} %param.5) | copy-start | bytes 786436
  90.2 1.2 %copy-start.35 = (f32[32,16,128]{2,0,1:T(8,128)S(1)}, f32[32,16,128]{2,0,1:T(8,128)}, u32[]{:S(2)}) copy-start(f32[32,16,128]{2,0,1:T(8,128)} %get-tuple-element.11) | copy-start | bytes 786436
  92.7 6.0 %collective-permute-start.12 = (f32[3,32,1,128]{3,1,2,0:T(8,128)S(1)}, f32[3,32,1,128]{3,1,2,0:T(8,128)S(1)}, u32[]{:S(2)}, u32[]{:S(2)}) collective-permute-start(f32[3,32,1,128]{3,1,2,0:T(8,128)S(1)} %get-tuple-element.20), channel_id=1, source_target_pairs={{0,8},{8,16},{16,24},{24,32},{32,40},{40,48},{48,56},{56,64},{64,7... | collective-permute-start | bytes 147464 | tf_op jit(solution)/shard_map/ppermute | solution.py:20
  94.6 9.3 %collective-permute-start.13 = (f32[3,32,1,128]{3,1,2,0:T(8,128)S(1)}, f32[3,32,1,128]{3,1,2,0:T(8,128)S(1)}, u32[]{:S(2)}, u32[]{:S(2)}) collective-permute-start(f32[3,32,1,128]{3,1,2,0:T(8,128)S(1)} %get-tuple-element.21), channel_id=1, source_target_pairs={{8,0},{16,8},{24,16},{32,24},{40,32},{48,40},{56,48},{64,56},{72,6... | collective-permute-start | bytes 147464 | tf_op jit(solution)/shard_map/ppermute | solution.py:21
  104.8 4.8 %collective-permute-start.15 = (f32[3,32,18,1]{1,2,3,0:T(8,128)S(1)}, f32[3,32,18,1]{1,2,3,0:T(8,128)S(1)}, u32[]{:S(2)}, u32[]{:S(2)}) collective-permute-start(f32[3,32,18,1]{1,2,3,0:T(8,128)S(1)} %copy.120), channel_id=1, source_target_pairs={{1,0},{2,1},{3,2},{4,3},{5,4},{6,5},{7,6},{9,8},{10,9},{11,10},{12... | collective-permute-start | bytes 20744 | tf_op jit(solution)/shard_map/ppermute | solution.py:21
  107.2 5.3 %collective-permute-start.14 = (f32[3,32,18,1]{1,2,3,0:T(8,128)S(1)}, f32[3,32,18,1]{1,2,3,0:T(8,128)S(1)}, u32[]{:S(2)}, u32[]{:S(2)}) collective-permute-start(f32[3,32,18,1]{1,2,3,0:T(8,128)S(1)} %copy.119), channel_id=1, source_target_pairs={{0,1},{1,2},{2,3},{3,4},{4,5},{5,6},{6,7},{8,9},{9,10},{10,11},{11... | collective-permute-start | bytes 20744 | tf_op jit(solution)/shard_map/ppermute | solution.py:20
  112.9 1.0 copy-start.14
  112.9 1.1 copy-start.17
  112.9 1.2 copy-start.20
  112.9 1.2 %copy-start.23 = (f32[32,16,128]{2,0,1:T(8,128)S(1)}, f32[32,16,128]{2,0,1:T(8,128)}, u32[]{:S(2)}) copy-start(f32[32,16,128]{2,0,1:T(8,128)} %get-tuple-element.30) | copy-start | bytes 786436
  112.9 1.3 %copy-start.26 = (f32[32,16,128]{2,0,1:T(8,128)S(1)}, f32[32,16,128]{2,0,1:T(8,128)}, u32[]{:S(2)}) copy-start(f32[32,16,128]{2,0,1:T(8,128)} %get-tuple-element.31) | copy-start | bytes 786436
  112.9 1.4 %copy-start.29 = (f32[32,16,128]{2,0,1:T(8,128)S(1)}, f32[32,16,128]{2,0,1:T(8,128)}, u32[]{:S(2)}) copy-start(f32[32,16,128]{2,0,1:T(8,128)} %get-tuple-element.32) | copy-start | bytes 786436
  (5 other events, 5.0 us)
where the time goes:
time: 118 us; the launch traced here: 117 us
  starting transfers between devices  51.3 us (43%)
  waiting for transfers between devices  41.8 us (35%)
  other arithmetic  11 us (9%)
  local copies, waits for them, and re-layouts  10.8 us (9%)
    ppermute x8, waiting for transfers between devices, with_halo(): after = lax.ppermute(initial, axis, down)  22.6 us
    ppermute x8, starting transfers between devices, with_halo(): after = lax.ppermute(initial, axis, down)  21.7 us
    ppermute x8, starting transfers between devices, with_halo(): before = lax.ppermute(last, axis, up)  19.5 us
    ppermute x8, waiting for transfers between devices, with_halo(): before = lax.ppermute(last, axis, up)  11.3 us
    all_to_all x1, starting transfers between devices, body(): lax.all_to_all(moving_slab, 'row', split_axis=1, concat_axis=0, tiled=True)  10.2 us
    all_to_all x1, waiting for transfers between devices, body(): lax.all_to_all(moving_slab, 'row', split_axis=1, concat_axis=0, tiled=True)  7.97 us
    unnamed x81, local copies, waits for them, and re-layouts  5.77 us
    add x3, other arithmetic, smooth(): return centre + smooth_rate * centre_tissue * flow  3.44 us
  transfers between devices with their start and end apart: 17, of which 11 were waited for; matrix products, arithmetic and copies ran while one was open for 5% of the time, Pallas kernels for 0%

commit v1 on v0

v1 whole, which is shorter than its diff:
```python
import jax
import jax.numpy as jnp
from jax import lax
from jax.experimental import pallas as pl
from jax.experimental.pallas import tpu as pltpu
from jax.sharding import PartitionSpec as P

ITERS = 3
pull_rate = 1.0
smooth_rate = 0.16

NZ = 32
BY = 16
HY = 8
RY = BY + HY
LX = 128
EX = LX // NZ
ZG = 8

VMEM = pltpu.VMEM
f32 = jnp.float32


def iota(shape, dim):
    return lax.broadcasted_iota(jnp.int32, shape, dim)


def cut_kernel(slab_ref, out_ref):
    count = slab_ref.shape[0]
    low = iota((HY, LX), 0) < HY // 2
    zero = jnp.zeros((HY, LX), f32)
    for i in range(count):
        after = slab_ref[i + 1, 0:HY] if i + 1 < count else zero
        before = slab_ref[i - 1, HY:BY] if i else zero
        out_ref[i, 0:BY] = slab_ref[i]
        out_ref[i, BY:RY] = jnp.where(low, after, before)


def cut(slab):
    count = slab.shape[1] // BY
    return pl.pallas_call(
        cut_kernel,
        out_shape=jax.ShapeDtypeStruct((count, RY, LX), f32),
        in_specs=[pl.BlockSpec(memory_space=VMEM)],
        out_specs=pl.BlockSpec(memory_space=VMEM),
        name="cut",
    )(slab.reshape(count, BY, LX))


def pack_kernel(moving_ref, fixed_ref, field_ref, halo_ref, left_ref, right_ref):
    group = iota((RY, LX), 1) // EX

    def rows(which, z):
        if which == 4:
            return moving_ref[z]
        core = fixed_ref[z] if which == 3 else field_ref[which, z]
        return jnp.concatenate([core, halo_ref[which, z]], axis=0)

    for which in range(5):

        def step(z, packs):
            left, right = packs
            turned = pltpu.roll(rows(which, z), 4 * z + 4, 1)
            right = jnp.where(group == z, turned, right)
            left = jnp.where(group == lax.rem(z + 1, NZ), turned, left)
            return left, right

        zero = jnp.zeros((RY, LX), f32)
        left, right = lax.fori_loop(0, NZ, step, (zero, zero), unroll=4)
        left_ref[which] = pltpu.roll(left, LX - EX, 1)
        right_ref[which] = right


def pack(moving, fixed, field, halo):
    shape = jax.ShapeDtypeStruct((5, RY, LX), f32)
    return pl.pallas_call(
        pack_kernel,
        out_shape=(shape, shape),
        in_specs=[pl.BlockSpec(memory_space=VMEM)] * 4,
        out_specs=(pl.BlockSpec(memory_space=VMEM),) * 2,
        name="pack",
    )(moving, fixed, field, halo)


def recip(x):
    r = pl.reciprocal(x, approx=True)
    return r * (2.0 - x * r)


def attract(field, slopes, gap, energy, tissue):
    residual = gap - (slopes[0] * field[0] + slopes[1] * field[1] + slopes[2] * field[2])
    rate = pull_rate * tissue * residual * recip(energy + residual * residual)
    return [field[c] + rate * slopes[c] for c in range(3)]


def strip_neighbours(packs):
    lane = iota((RY, LX), 1)
    j = lane % EX
    first, last = j == 0, j == EX - 1
    low, high = lane < EX, lane >= LX - EX
    out = []
    for inner, pair in ((0, (0, 1)), (1, (0, 1)), (0, (2, 3)), (1, (2, 3))):
        a, b = packs[pair[0]], packs[pair[1]]
        own = b if inner else a
        before = jnp.where(first, pltpu.roll(a, LX - EX + 1, 1), pltpu.roll(b, 1, 1)) if inner else pltpu.roll(a, 1, 1)
        after = pltpu.roll(b, LX - 1, 1) if inner else jnp.where(last, pltpu.roll(b, EX - 1, 1), pltpu.roll(a, LX - 1, 1))
        out.append(
            (
                jnp.where(high, 0.0, pltpu.roll(own, LX - EX, 1)),
                jnp.where(low, 0.0, pltpu.roll(own, EX, 1)),
                pltpu.roll(own, RY - 1, 0),
                pltpu.roll(own, 1, 0),
                after,
                before,
            )
        )
    return out


def beside(packs):
    j = iota((RY, LX), 1) % EX
    return jnp.where(j == 2, pltpu.roll(packs[0], LX - 1, 1), pltpu.roll(packs[3], 1, 1))


def total(neighbours):
    up, down, after_y, before_y, after_x, before_x = neighbours
    return ((up + down) + (after_y + before_y)) + (after_x + before_x)


def main_kernel(
    tissue_ref,
    inside_ref,
    moving_ref,
    fixed_ref,
    field_ref,
    halo_ref,
    own_left_ref,
    own_right_ref,
    got_left_ref,
    got_right_ref,
    out_ref,
    slope_ref,
    energy_ref,
    gap_ref,
    ping_ref,
    pong_ref,
    beside_ref,
    tissue_rows_ref,
    keep_ref,
):
    lane = iota((RY, LX), 1)
    row = iota((RY, LX), 0)
    at_left, at_right = lane == 0, lane == LX - 1
    groups = NZ // ZG

    def rows_of(column, group):
        def at(k):
            return tissue_ref[(group * 3 + k) * 3 + column]

        return jnp.where(row < BY, at(1), jnp.where(row < BY + HY // 2, at(2), at(0)))

    cells = [rows_of(1, g) for g in range(groups)]
    flat = []
    for g in range(groups):
        own = cells[g]
        tissue_rows_ref[g] = own
        across = jnp.where(at_left, rows_of(0, g), own) + jnp.where(at_right, rows_of(2, g), own)
        flat.append(across + pltpu.roll(own, 1, 0) + pltpu.roll(own, RY - 1, 0))
    zero = jnp.zeros((RY, LX), f32)
    for g in range(groups):
        below = cells[g - 1] if g else zero
        above = cells[g + 1] if g + 1 < groups else zero
        keep_ref[3 * g] = 1.0 - smooth_rate * cells[g] * (flat[g] + below + cells[g])
        keep_ref[3 * g + 1] = 1.0 - smooth_rate * cells[g] * (flat[g] + cells[g] + cells[g])
        keep_ref[3 * g + 2] = 1.0 - smooth_rate * cells[g] * (flat[g] + cells[g] + above)

    def strips(which, edge=None):
        a, d = got_left_ref[which], got_right_ref[which]
        if edge is not None:
            a, d = a * edge[0], d * edge[1]
        return [a, own_left_ref[which], own_right_ref[which], d]

    strip_tissue = []
    for column in (0, 1, 1, 2):
        cell = rows_of(column, groups - 1)
        for g in range(groups - 2, -1, -1):
            cell = jnp.where(lane < (g + 1) * ZG * EX, rows_of(column, g), cell)
        strip_tissue.append(cell)
    strip_keep = [
        1.0 - smooth_rate * t * total(n) for t, n in zip(strip_tissue, strip_neighbours(strip_tissue))
    ]
    strip_moving = strips(4, (inside_ref[0], inside_ref[1]))
    strip_slopes, strip_energy = [], []
    for up, down, after_y, before_y, after_x, before_x in strip_neighbours(strip_moving):
        s = [0.5 * (up - down), 0.5 * (after_y - before_y), 0.5 * (after_x - before_x)]
        strip_slopes.append(s)
        strip_energy.append(s[0] * s[0] + s[1] * s[1] + s[2] * s[2] + 0.5)
    strip_gap = [f - m for f, m in zip(strips(3), strip_moving)]
    strip_field = [[x * t for x, t in zip(strips(c), strip_tissue)] for c in range(3)]

    def strip_attract():
        parts = [
            attract([strip_field[c][k] for c in range(3)], strip_slopes[k], strip_gap[k], strip_energy[k], strip_tissue[k])
            for k in range(4)
        ]
        return [[parts[k][c] for k in range(4)] for c in range(3)]

    def strip_smooth(pulled):
        out = []
        for c in range(3):
            near = strip_neighbours(pulled[c])
            out.append(
                [strip_keep[k] * pulled[c][k] + smooth_rate * strip_tissue[k] * total(near[k]) for k in range(4)]
            )
        return out

    def edges(values, side, rows=RY):
        before = jnp.where(at_left[:rows], side, pltpu.roll(values, 1, 1))
        after = jnp.where(at_right[:rows], side, pltpu.roll(values, LX - 1, 1))
        return before, after

    def side_at(c, z):
        return pltpu.roll(beside_ref[c], LX - 2 - EX * z, 1)

    beside_ref[0] = beside(strip_moving)
    for ref in (ping_ref, pong_ref):
        for c in range(3):
            ref[c, 0] = zero
            ref[c, NZ + 1] = zero

    def first(z, carry):
        m = moving_ref[z]
        above = jnp.where(z < NZ - 1, moving_ref[jnp.minimum(z + 1, NZ - 1)], 0.0)
        below = jnp.where(z > 0, moving_ref[jnp.maximum(z - 1, 0)], 0.0)
        before, after = edges(m, side_at(0, z))
        s = [
            0.5 * (above - below),
            0.5 * (pltpu.roll(m, RY - 1, 0) - pltpu.roll(m, 1, 0)),
            0.5 * (after - before),
        ]
        energy = s[0] * s[0] + s[1] * s[1] + s[2] * s[2] + 0.5
        gap = jnp.concatenate([fixed_ref[z], halo_ref[3, z]], axis=0) - m
        t = tissue_rows_ref[z // ZG]
        field = [t * jnp.concatenate([field_ref[c, z], halo_ref[c, z]], axis=0) for c in range(3)]
        pulled = attract(field, s, gap, energy, t)
        for c in range(3):
            slope_ref[c, z] = s[c]
            ping_ref[c, z + 1] = pulled[c]
        energy_ref[z] = energy
        gap_ref[z] = gap
        return carry

    lax.fori_loop(0, NZ, first, 0, unroll=2)

    def smoothed(src, z, c, t, keep, rows):
        p = src[c, z + 1]
        before, after = edges(p[:rows], side_at(c, z)[:rows], rows)
        y = pltpu.roll(p, RY - 1, 0) + pltpu.roll(p, 1, 0)
        around = ((src[c, z + 2][:rows] + src[c, z][:rows]) + y[:rows]) + (before + after)
        return keep * p[:rows] + (smooth_rate * t) * around

    def keep_at(z):
        g, k = z // ZG, z % ZG
        return keep_ref[3 * g + jnp.where(k == 0, 0, jnp.where(k == ZG - 1, 2, 1))]

    src, dst = ping_ref, pong_ref
    for sweep in range(ITERS):
        pulled = strip_attract()
        for c in range(3):
            beside_ref[c] = beside(pulled[c])
        if sweep < ITERS - 1:
            strip_field = strip_smooth(pulled)

            def middle(z, carry, src=src, dst=dst):
                t = tissue_rows_ref[z // ZG]
                keep = keep_at(z)
                field = [smoothed(src, z, c, t, keep, RY) for c in range(3)]
                s = [slope_ref[c, z] for c in range(3)]
                pulled = attract(field, s, gap_ref[z], energy_ref[z], t)
                for c in range(3):
                    dst[c, z + 1] = pulled[c]
                return carry

            lax.fori_loop(0, NZ, middle, 0, unroll=2)
            src, dst = dst, src
        else:

            def final(z, carry, src=src):
                t = tissue_rows_ref[z // ZG][:BY]
                keep = keep_at(z)[:BY]
                for c in range(3):
                    out_ref[c, z] = smoothed(src, z, c, t, keep, BY)
                return carry

            lax.fori_loop(0, NZ, final, 0, unroll=2)


def register(tissue, inside, moving, fixed, field, halo, own_left, own_right, got_left, got_right):
    smem = pl.BlockSpec(memory_space=pltpu.SMEM)
    vmem = pl.BlockSpec(memory_space=VMEM)
    return pl.pallas_call(
        main_kernel,
        out_shape=jax.ShapeDtypeStruct((3, NZ, BY, LX), f32),
        in_specs=[smem, smem] + [vmem] * 8,
        out_specs=vmem,
        scratch_shapes=[
            VMEM((3, NZ, RY, LX), f32),
            VMEM((NZ, RY, LX), f32),
            VMEM((NZ, RY, LX), f32),
            VMEM((3, NZ + 2, RY, LX), f32),
            VMEM((3, NZ + 2, RY, LX), f32),
            VMEM((3, RY, LX), f32),
            VMEM((NZ // ZG, RY, LX), f32),
            VMEM((3 * NZ // ZG, RY, LX), f32),
        ],
        compiler_params=pltpu.CompilerParams(vmem_limit_bytes=24 * 2**20),
        name="register",
    )(tissue, inside, moving, fixed, field, halo, own_left, own_right, got_left, got_right)


def turn(x, axis, by):
    size = lax.axis_size(axis)
    return lax.ppermute(x, axis, [(i, (i + by) % size) for i in range(size)])


def body(moving_slab, fixed_image, start_field, tissue_mask):
    row = lax.axis_index("row")
    col = lax.axis_index("col")
    blocks = cut(moving_slab)
    moving = lax.all_to_all(blocks, "row", split_axis=0, concat_axis=0, tiled=True)

    state = jnp.concatenate([start_field, fixed_image[None]], axis=0)
    after = turn(state[:, :, 0 : HY // 2], "row", -1)
    before = turn(state[:, :, BY - HY // 2 :], "row", 1)
    halo = jnp.concatenate([after, before], axis=2)

    padded = jnp.pad(tissue_mask, ((0, 0), (1, 1), (1, 1))).astype(f32)
    tissue = lax.dynamic_slice(padded, (0, row, col), (NZ // ZG, 3, 3)).reshape(-1)
    inside = jnp.stack([col > 0, col < lax.axis_size("col") - 1]).astype(f32)

    own_left, own_right = pack(moving, fixed_image, start_field, halo)
    got_left = turn(own_right, "col", 1)
    got_right = turn(own_left, "col", -1)
    return register(
        tissue, inside, moving, fixed_image, start_field, halo, own_left, own_right, got_left, got_right
    )


def solution(mesh):
    in_specs = (P("row", None, "col"), P(None, "row", "col"), P(None, None, "row", "col"), P())
    out_specs = P(None, None, "row", "col")
    return jax.shard_map(body, mesh=mesh, in_specs=in_specs, out_specs=out_specs, check_vma=False)
```

time: 118 us -> 59.1 us (0.50)
  the two profiles are of different devices: /device:TPU:126 before, /device:TPU:1 now
where the time goes in v1:
time: 59.1 us; the launch traced here: 58 us
  starting transfers between devices  18.9 us (32%)
  Pallas kernels  18 us (30%)
  waiting for transfers between devices  16.3 us (28%)
  local copies, waits for them, and re-layouts  3.62 us (6%)
  other arithmetic  1.16 us (2%)
    ppermute x4, waiting for transfers between devices, turn(): return lax.ppermute(x, axis, [(i, (i + by) % size) for i in range(size)])  16.3 us
    all_to_all x1, starting transfers between devices, body(): lax.all_to_all(blocks, 'row', split_axis=0, concat_axis=0, tiled=True)  12 us
    pallas_call x1, Pallas kernels, register(): pl.pallas_call(main_kernel, out_shape=jax.ShapeDtypeStruct((3, NZ, BY, LX...  10.5 us
    ppermute x4, starting transfers between devices, turn(): return lax.ppermute(x, axis, [(i, (i + by) % size) for i in range(size)])  6.88 us
    pallas_call x1, Pallas kernels, pack(): pl.pallas_call(pack_kernel, out_shape=(shape, shape), in_specs=[pl.BlockS...  5.7 us
    unnamed x20, local copies, waits for them, and re-layouts  3.42 us
    pallas_call x1, Pallas kernels, cut(): pl.pallas_call(cut_kernel, out_shape=jax.ShapeDtypeStruct((count, RY, LX)...  1.8 us
  transfers between devices with their start and end apart: 5, of which 3 were waited for; matrix products, arithmetic and copies ran while one was open for 2% of the time, Pallas kernels for 0%

profile of v1, /device:TPU:1, one launch (start us, length us, event | category | flops | bytes accessed | tf_op | source)
XLA Modules:
  0.0 58.0 jit_solution(3819836184972829238)
XLA Ops:
  0.0 0.0 copy-start
  0.0 1.8 %cut.1 = f32[32,24,128]{2,1,0:T(8,128)} custom-call(f32[32,16,128]{2,1,0:T(8,128)} %bitcast.5), custom_call_target="tpu_custom_call" | custom-call | tf_op jit(solution)/shard_map/cut/pallas_call | solution.py:41
  1.8 0.0 copy-start.5
  1.8 12.0 %all-to-all-start = ((f32[32,24,128]{2,1,0:T(8,128)}), f32[32,24,128]{2,1,0:T(8,128)S(1)}, u32[]{:S(2)}, u32[]{:S(2)}) async-start(f32[32,24,128]{2,1,0:T(8,128)} %cut.1), calls=%async_computation | async-start | bytes 786432 | tf_op jit(solution)/shard_map/all_to_all | solution.py:330
  13.8 0.0 copy-done
  13.8 0.0 copy-done.5
  13.8 0.1 pad_maximum_fusion.2
  13.9 0.0 copy-start.9
  13.9 4.7 %collective-permute-start = (f32[4,32,4,128]{3,2,1,0:T(4,128)S(1)}, f32[4,32,4,128]{3,2,1,0:T(4,128)S(1)}, u32[]{:S(2)}, u32[]{:S(2)}) collective-permute-start(f32[4,32,4,128]{3,2,1,0:T(4,128)S(1)} %get-tuple-element.9), channel_id=1, source_target_pairs={{0,248},{8,0},{16,8},{24,16},{32,24},{40,32},{48,40},{56,48},{64,5... | collective-permute-start | bytes 786440 | tf_op jit(solution)/shard_map/ppermute | solution.py:323
  18.7 0.0 collective-permute-start.1
  18.7 0.0 copy-done.9
  18.7 0.1 fusion
  18.8 0.1 copy.6
  18.9 0.1 reshape.6.tissue_ref
  19.0 8.9 %collective-permute-done = f32[4,32,4,128]{3,2,1,0:T(4,128)S(1)} collective-permute-done((f32[4,32,4,128]{3,2,1,0:T(4,128)S(1)}, f32[4,32,4,128]{3,2,1,0:T(4,128)S(1)}, u32[]{:S(2)}, u32[]{:S(2)}) %collective-permute-start) | collective-permute-done | bytes 262176 | tf_op jit(solution)/shard_map/ppermute | solution.py:323
  27.8 5.4 %collective-permute-done.1 = f32[4,32,4,128]{3,2,1,0:T(4,128)S(1)} collective-permute-done((f32[4,32,4,128]{3,2,1,0:T(4,128)S(1)}, f32[4,32,4,128]{3,2,1,0:T(4,128)S(1)}, u32[]{:S(2)}, u32[]{:S(2)}) %collective-permute-start.1) | collective-permute-done | bytes 262176 | tf_op jit(solution)/shard_map/ppermute | solution.py:323
  33.3 0.9 %pad_maximum_fusion.halo_ref = f32[4,32,8,128]{3,2,1,0:T(8,128)} fusion(f32[4,32,4,128]{3,2,1,0:T(4,128)S(1)} %collective-permute-done.1, f32[4,32,4,128]{3,2,1,0:T(4,128)S(1)} %collective-permute-done), kind=kLoop, calls=%fused_computation | loop fusion | flops 131072 | bytes 1048576 | tf_op jit(solution)/shard_map/concatenate | solution.py:335
  34.2 0.0 copy-start.1
  34.2 0.0 copy-start.2
  34.2 0.0 copy-start.6
  34.2 0.0 all-to-all-done.moving_ref
  34.2 0.0 copy-start.3
  34.2 0.7 %copy-done.3 = f32[32,24,128]{2,1,0:T(8,128)} copy-done((f32[32,24,128]{2,1,0:T(8,128)}, f32[32,24,128]{2,1,0:T(8,128)S(1)}, u32[]{:S(2)}) %copy-start.3) | copy-done | bytes 393240
  34.9 5.7 %pack.1 = (f32[5,24,128]{2,1,0:T(8,128)}, f32[5,24,128]{2,1,0:T(8,128)}) custom-call(f32[32,24,128]{2,1,0:T(8,128)} %copy-done.3, f32[32,16,128]{2,1,0:T(8,128)} %fixed_ref.3, f32[3,32,16,128]{3,2,1,0:T(8,128)} %field_ref.3, f32[4,32,8,128]{3,2,1,0:T(8,128)} %pad_maximum_fusion.halo_ref), custom_call_target="tpu_custom_call" | custom-call | tf_op jit(solution)/shard_map/pack/pallas_call | solution.py:76
  40.6 1.0 %collective-permute-start.3 = (f32[5,24,128]{2,1,0:T(8,128)}, f32[5,24,128]{2,1,0:T(8,128)S(1)}, u32[]{:S(2)}, u32[]{:S(2)}) collective-permute-start(f32[5,24,128]{2,1,0:T(8,128)} %get-tuple-element.7.own_left_ref), channel_id=1, source_target_pairs={{0,7},{1,0},{2,1},{3,2},{4,3},{5,4},{6,5},{7,6},{8,15},{9,8},{10,9... | collective-permute-start | bytes 184328 | tf_op jit(solution)/shard_map/ppermute | solution.py:323
  41.6 1.2 %collective-permute-start.2 = (f32[5,24,128]{2,1,0:T(8,128)}, f32[5,24,128]{2,1,0:T(8,128)S(1)}, u32[]{:S(2)}, u32[]{:S(2)}) collective-permute-start(f32[5,24,128]{2,1,0:T(8,128)} %get-tuple-element.8.own_right_ref), channel_id=1, source_target_pairs={{0,1},{1,2},{2,3},{3,4},{4,5},{5,6},{6,7},{7,0},{8,9},{9,10},{10,1... | collective-permute-start | bytes 184328 | tf_op jit(solution)/shard_map/ppermute | solution.py:323
  42.8 0.1 add_convert_fusion.inside_ref
  42.9 2.0 %collective-permute-done.3.got_right_ref = f32[5,24,128]{2,1,0:T(8,128)S(1)} collective-permute-done((f32[5,24,128]{2,1,0:T(8,128)}, f32[5,24,128]{2,1,0:T(8,128)S(1)}, u32[]{:S(2)}, u32[]{:S(2)}) %collective-permute-start.3) | collective-permute-done | bytes 61472 | tf_op jit(solution)/shard_map/ppermute | solution.py:323
  44.9 0.0 collective-permute-done.2.got_left_ref
  44.9 0.0 copy-done.1
  44.9 0.0 copy-done.2
  44.9 0.0 copy-done.6
  44.9 0.0 copy-start.4
  44.9 1.0 %copy-done.4 = f32[32,24,128]{2,1,0:T(8,128)S(1)} copy-done((f32[32,24,128]{2,1,0:T(8,128)S(1)}, f32[32,24,128]{2,1,0:T(8,128)}, u32[]{:S(2)}) %copy-start.4) | copy-done | bytes 393240
  45.9 0.0 copy-start.7
  45.9 0.8 %copy-done.7 = f32[5,24,128]{2,1,0:T(8,128)S(1)} copy-done((f32[5,24,128]{2,1,0:T(8,128)S(1)}, f32[5,24,128]{2,1,0:T(8,128)}, u32[]{:S(2)}) %copy-start.7) | copy-done | bytes 61464
  46.7 0.0 copy-start.8
  46.8 0.8 %copy-done.8 = f32[5,24,128]{2,1,0:T(8,128)S(1)} copy-done((f32[5,24,128]{2,1,0:T(8,128)S(1)}, f32[5,24,128]{2,1,0:T(8,128)}, u32[]{:S(2)}) %copy-start.8) | copy-done | bytes 61464
  47.6 10.5 %register.1 = f32[3,32,16,128]{3,2,1,0:T(8,128)} custom-call(f32[36]{0:T(128)S(1)} %reshape.6.tissue_ref, f32[2]{0:T(128)S(1)} %add_convert_fusion.inside_ref, f32[32,24,128]{2,1,0:T(8,128)S(1)} %copy-done.4, f32[32,16,128]{2,1,0:T(8,128)S(1)} %copy-done.6, f32[3,32,16,128]{3,2,1,0:T(8,128)S(1)} %copy-done.1, f32[4,32,8,128]{3,2,1,0:T(8,128)S(1)} %copy-done.2, ...), custom_call_target="tpu_custom_call" | custom-call | tf_op jit(solution)/shard_map/register/pallas_call | solution.py:301
Async XLA Ops:
  0.0 13.8 %copy-start = (f32[3,32,16,128]{3,2,1,0:T(8,128)S(1)}, f32[3,32,16,128]{3,2,1,0:T(8,128)}, u32[]{:S(2)}) copy-start(f32[3,32,16,128]{3,2,1,0:T(8,128)} %field_ref.3) | copy-start | bytes 2359300
  1.8 12.0 %copy-start.5 = (f32[32,16,128]{2,1,0:T(8,128)S(1)}, f32[32,16,128]{2,1,0:T(8,128)}, u32[]{:S(2)}) copy-start(f32[32,16,128]{2,1,0:T(8,128)} %fixed_ref.3) | copy-start | bytes 786436
  1.8 32.4 %all-to-all-start = ((f32[32,24,128]{2,1,0:T(8,128)}), f32[32,24,128]{2,1,0:T(8,128)S(1)}, u32[]{:S(2)}, u32[]{:S(2)}) async-start(f32[32,24,128]{2,1,0:T(8,128)} %cut.1), calls=%async_computation | async-start | bytes 786432 | tf_op jit(solution)/shard_map/all_to_all | solution.py:330
  13.9 4.7 %copy-start.9 = (s32[4,32,8]{1,2,0:T(8,128)S(1)}, s32[4,32,8]{1,2,0:T(8,128)}, u32[]{:S(2)}) copy-start(s32[4,32,8]{1,2,0:T(8,128)} %param.7) | copy-start | bytes 12292
  13.9 13.9 %collective-permute-start = (f32[4,32,4,128]{3,2,1,0:T(4,128)S(1)}, f32[4,32,4,128]{3,2,1,0:T(4,128)S(1)}, u32[]{:S(2)}, u32[]{:S(2)}) collective-permute-start(f32[4,32,4,128]{3,2,1,0:T(4,128)S(1)} %get-tuple-element.9), channel_id=1, source_target_pairs={{0,248},{8,0},{16,8},{24,16},{32,24},{40,32},{48,40},{56,48},{64,5... | collective-permute-start | bytes 786440 | tf_op jit(solution)/shard_map/ppermute | solution.py:323
  18.7 14.6 %collective-permute-start.1 = (f32[4,32,4,128]{3,2,1,0:T(4,128)S(1)}, f32[4,32,4,128]{3,2,1,0:T(4,128)S(1)}, u32[]{:S(2)}, u32[]{:S(2)}) collective-permute-start(f32[4,32,4,128]{3,2,1,0:T(4,128)S(1)} %get-tuple-element.10), channel_id=1, source_target_pairs={{0,8},{8,16},{16,24},{24,32},{32,40},{40,48},{48,56},{56,64},{64,7... | collective-permute-start | bytes 786440 | tf_op jit(solution)/shard_map/ppermute | solution.py:323
  34.2 10.7 %copy-start.1 = (f32[3,32,16,128]{3,2,1,0:T(8,128)S(1)}, f32[3,32,16,128]{3,2,1,0:T(8,128)}, u32[]{:S(2)}) copy-start(f32[3,32,16,128]{3,2,1,0:T(8,128)} %field_ref.3) | copy-start | bytes 2359300
  34.2 10.7 %copy-start.2 = (f32[4,32,8,128]{3,2,1,0:T(8,128)S(1)}, f32[4,32,8,128]{3,2,1,0:T(8,128)}, u32[]{:S(2)}) copy-start(f32[4,32,8,128]{3,2,1,0:T(8,128)} %pad_maximum_fusion.halo_ref) | copy-start | bytes 1572868
  34.2 10.7 %copy-start.6 = (f32[32,16,128]{2,1,0:T(8,128)S(1)}, f32[32,16,128]{2,1,0:T(8,128)}, u32[]{:S(2)}) copy-start(f32[32,16,128]{2,1,0:T(8,128)} %fixed_ref.3) | copy-start | bytes 786436
  34.2 0.8 %copy-start.3 = (f32[32,24,128]{2,1,0:T(8,128)}, f32[32,24,128]{2,1,0:T(8,128)S(1)}, u32[]{:S(2)}) copy-start(f32[32,24,128]{2,1,0:T(8,128)S(1)} %all-to-all-done.moving_ref) | copy-start | bytes 1179652
  40.6 4.3 %collective-permute-start.3 = (f32[5,24,128]{2,1,0:T(8,128)}, f32[5,24,128]{2,1,0:T(8,128)S(1)}, u32[]{:S(2)}, u32[]{:S(2)}) collective-permute-start(f32[5,24,128]{2,1,0:T(8,128)} %get-tuple-element.7.own_left_ref), channel_id=1, source_target_pairs={{0,7},{1,0},{2,1},{3,2},{4,3},{5,4},{6,5},{7,6},{8,15},{9,8},{10,9... | collective-permute-start | bytes 184328 | tf_op jit(solution)/shard_map/ppermute | solution.py:323
  41.6 3.3 %collective-permute-start.2 = (f32[5,24,128]{2,1,0:T(8,128)}, f32[5,24,128]{2,1,0:T(8,128)S(1)}, u32[]{:S(2)}, u32[]{:S(2)}) collective-permute-start(f32[5,24,128]{2,1,0:T(8,128)} %get-tuple-element.8.own_right_ref), channel_id=1, source_target_pairs={{0,1},{1,2},{2,3},{3,4},{4,5},{5,6},{6,7},{7,0},{8,9},{9,10},{10,1... | collective-permute-start | bytes 184328 | tf_op jit(solution)/shard_map/ppermute | solution.py:323
  44.9 1.0 %copy-start.4 = (f32[32,24,128]{2,1,0:T(8,128)S(1)}, f32[32,24,128]{2,1,0:T(8,128)}, u32[]{:S(2)}) copy-start(f32[32,24,128]{2,1,0:T(8,128)} %copy-done.3) | copy-start | bytes 1179652
  45.9 0.8 %copy-start.7 = (f32[5,24,128]{2,1,0:T(8,128)S(1)}, f32[5,24,128]{2,1,0:T(8,128)}, u32[]{:S(2)}) copy-start(f32[5,24,128]{2,1,0:T(8,128)} %get-tuple-element.7.own_left_ref) | copy-start | bytes 184324
  46.7 0.8 %copy-start.8 = (f32[5,24,128]{2,1,0:T(8,128)S(1)}, f32[5,24,128]{2,1,0:T(8,128)}, u32[]{:S(2)}) copy-start(f32[5,24,128]{2,1,0:T(8,128)} %get-tuple-element.8.own_right_ref) | copy-start | bytes 184324

commit v2 on v1

--- a/solution.py
+++ b/solution.py
@@ -43,6 +43,7 @@
         out_shape=jax.ShapeDtypeStruct((count, RY, LX), f32),
         in_specs=[pl.BlockSpec(memory_space=VMEM)],
         out_specs=pl.BlockSpec(memory_space=VMEM),
+        compiler_params=pltpu.CompilerParams(vmem_limit_bytes=4 * 2**20),
         name="cut",
     )(slab.reshape(count, BY, LX))
 
@@ -66,7 +67,7 @@
             return left, right
 
         zero = jnp.zeros((RY, LX), f32)
-        left, right = lax.fori_loop(0, NZ, step, (zero, zero), unroll=4)
+        left, right = lax.fori_loop(0, NZ, step, (zero, zero), unroll=NZ)
         left_ref[which] = pltpu.roll(left, LX - EX, 1)
         right_ref[which] = right
 
@@ -78,6 +79,7 @@
         out_shape=(shape, shape),
         in_specs=[pl.BlockSpec(memory_space=VMEM)] * 4,
         out_specs=(pl.BlockSpec(memory_space=VMEM),) * 2,
+        compiler_params=pltpu.CompilerParams(vmem_limit_bytes=8 * 2**20),
         name="pack",
     )(moving, fixed, field, halo)
 
@@ -250,7 +252,7 @@
         gap_ref[z] = gap
         return carry
 
-    lax.fori_loop(0, NZ, first, 0, unroll=2)
+    lax.fori_loop(0, NZ, first, 0, unroll=NZ)
 
     def smoothed(src, z, c, t, keep, rows):
         p = src[c, z + 1]
@@ -281,7 +283,7 @@
                     dst[c, z + 1] = pulled[c]
                 return carry
 
-            lax.fori_loop(0, NZ, middle, 0, unroll=2)
+            lax.fori_loop(0, NZ, middle, 0, unroll=NZ)
             src, dst = dst, src
         else:
 
@@ -292,7 +294,7 @@
                     out_ref[c, z] = smoothed(src, z, c, t, keep, BY)
                 return carry
 
-            lax.fori_loop(0, NZ, final, 0, unroll=2)
+            lax.fori_loop(0, NZ, final, 0, unroll=NZ)
 
 
 def register(tissue, inside, moving, fixed, field, halo, own_left, own_right, got_left, got_right):
@@ -313,7 +315,7 @@
             VMEM((NZ // ZG, RY, LX), f32),
             VMEM((3 * NZ // ZG, RY, LX), f32),
         ],
-        compiler_params=pltpu.CompilerParams(vmem_limit_bytes=24 * 2**20),
+        compiler_params=pltpu.CompilerParams(vmem_limit_bytes=16 * 2**20),
         name="register",
     )(tissue, inside, moving, fixed, field, halo, own_left, own_right, got_left, got_right)
 

time: 59.1 us -> 44.4 us (0.75)
  Pallas kernels: 18 us -> 6.83 us
  local copies, waits for them, and re-layouts: 3.62 us -> 1.24 us
  other arithmetic: 1.16 us -> 0.37 us
    pallas_call x1, Pallas kernels: 10.5 us -> 5.09 us  [register(): pl.pallas_call(main_kernel, out_shape=jax.ShapeDtypeStruct((3, NZ, BY, LX...]
    pallas_call x1, Pallas kernels: 5.7 us -> 0.97 us  [pack(): pl.pallas_call(pack_kernel, out_shape=(shape, shape), in_specs=[pl.BlockS...]
    unnamed x20 -> x8, local copies, waits for them, and re-layouts: 3.42 us -> 1.04 us
    pallas_call x1, Pallas kernels: 1.8 us -> 0.77 us  [cut(): pl.pallas_call(cut_kernel, out_shape=jax.ShapeDtypeStruct((count, RY, LX)...]
    concatenate x1, other arithmetic: 0.9 us -> 0.11 us  [body(): halo = jnp.concatenate([after, before], axis=2)]
  transfers between devices with their start and end apart: 5 -> 5, of which waited for: 3 -> 3; matrix products, arithmetic and copies ran while one was open for 2% -> 1% of each run, Pallas kernels for 0% -> 0%
where the time goes in v2:
time: 44.4 us; the launch traced here: 43.5 us
  starting transfers between devices  18.9 us (43%)
  waiting for transfers between devices  16.1 us (36%)
  Pallas kernels  6.83 us (15%)
  local copies, waits for them, and re-layouts  1.24 us (3%)
    ppermute x4, waiting for transfers between devices, turn(): return lax.ppermute(x, axis, [(i, (i + by) % size) for i in range(size)])  16.1 us
    all_to_all x1, starting transfers between devices, body(): lax.all_to_all(blocks, 'row', split_axis=0, concat_axis=0, tiled=True)  12 us
    ppermute x4, starting transfers between devices, turn(): return lax.ppermute(x, axis, [(i, (i + by) % size) for i in range(size)])  6.88 us
    pallas_call x1, Pallas kernels, register(): pl.pallas_call(main_kernel, out_shape=jax.ShapeDtypeStruct((3, NZ, BY, LX...  5.09 us
    unnamed x8, local copies, waits for them, and re-layouts  1.04 us
    pallas_call x1, Pallas kernels, pack(): pl.pallas_call(pack_kernel, out_shape=(shape, shape), in_specs=[pl.BlockS...  0.97 us
  transfers between devices with their start and end apart: 5, of which 3 were waited for; matrix products, arithmetic and copies ran while one was open for 1% of the time, Pallas kernels for 0%

profile of v2, /device:TPU:1, one launch (start us, length us, event | category | flops | bytes accessed | tf_op | source)
XLA Modules:
  0.0 43.5 jit_solution(14194167857482226982)
XLA Ops:
  0.0 0.0 copy-start
  0.0 0.0 copy-start.2
  0.0 1.0 %copy-done.2 = f32[1,512,128]{2,1,0:T(8,128)S(1)} copy-done((f32[1,512,128]{2,1,0:T(8,128)S(1)}, f32[1,512,128]{2,1,0:T(8,128)}, u32[]{:S(2)}) %copy-start.2) | copy-done | bytes 262168
  1.0 0.8 %cut.1 = f32[32,24,128]{2,1,0:T(8,128)} custom-call(f32[32,16,128]{2,1,0:T(8,128)S(1)} %bitcast.5), custom_call_target="tpu_custom_call" | custom-call | tf_op jit(solution)/shard_map/cut/pallas_call | solution.py:41
  1.8 0.0 copy-start.1
  1.8 12.0 %all-to-all-start = ((f32[32,24,128]{2,1,0:T(8,128)}), f32[32,24,128]{2,1,0:T(8,128)S(1)}, u32[]{:S(2)}, u32[]{:S(2)}) async-start(f32[32,24,128]{2,1,0:T(8,128)} %cut.1), calls=%async_computation | async-start | bytes 786432 | tf_op jit(solution)/shard_map/all_to_all | solution.py:332
  13.8 0.0 copy-done
  13.8 0.0 copy-done.1
  13.8 0.1 pad_maximum_fusion.2
  13.9 0.0 copy-start.3
  13.9 4.7 %collective-permute-start = (f32[4,32,4,128]{3,2,1,0:T(4,128)S(1)}, f32[4,32,4,128]{3,2,1,0:T(4,128)S(1)}, u32[]{:S(2)}, u32[]{:S(2)}) collective-permute-start(f32[4,32,4,128]{3,2,1,0:T(4,128)S(1)} %get-tuple-element.9), channel_id=1, source_target_pairs={{0,248},{8,0},{16,8},{24,16},{32,24},{40,32},{48,40},{56,48},{64,5... | collective-permute-start | bytes 786440 | tf_op jit(solution)/shard_map/ppermute | solution.py:325
  18.7 0.0 collective-permute-start.1
  18.7 0.0 copy-done.3
  18.7 0.1 fusion
  18.8 0.1 copy.6
  18.9 0.1 reshape.6.tissue_ref
  19.0 8.9 %collective-permute-done = f32[4,32,4,128]{3,2,1,0:T(4,128)S(1)} collective-permute-done((f32[4,32,4,128]{3,2,1,0:T(4,128)S(1)}, f32[4,32,4,128]{3,2,1,0:T(4,128)S(1)}, u32[]{:S(2)}, u32[]{:S(2)}) %collective-permute-start) | collective-permute-done | bytes 262176 | tf_op jit(solution)/shard_map/ppermute | solution.py:325
  27.8 5.4 %collective-permute-done.1 = f32[4,32,4,128]{3,2,1,0:T(4,128)S(1)} collective-permute-done((f32[4,32,4,128]{3,2,1,0:T(4,128)S(1)}, f32[4,32,4,128]{3,2,1,0:T(4,128)S(1)}, u32[]{:S(2)}, u32[]{:S(2)}) %collective-permute-start.1) | collective-permute-done | bytes 262176 | tf_op jit(solution)/shard_map/ppermute | solution.py:325
  33.3 0.1 pad_maximum_fusion.halo_ref
  33.4 0.0 all-to-all-done.moving_ref
  33.4 1.0 %pack.1 = (f32[5,24,128]{2,1,0:T(8,128)S(1)}, f32[5,24,128]{2,1,0:T(8,128)S(1)}) custom-call(f32[32,24,128]{2,1,0:T(8,128)S(1)} %all-to-all-done.moving_ref, f32[32,16,128]{2,1,0:T(8,128)S(1)} %copy-done.1, f32[3,32,16,128]{3,2,1,0:T(8,128)S(1)} %copy-done, f32[4,32,8,128]{3,2,1,0:T(8,128)S(1)} %pad_maximum_fusion.halo_ref), custom_call_target="tpu_custom_call" | custom-call | tf_op jit(solution)/shard_map/pack/pallas_call | solution.py:77
  34.4 1.0 %collective-permute-start.3 = (f32[5,24,128]{2,1,0:T(8,128)S(1)}, f32[5,24,128]{2,1,0:T(8,128)S(1)}, u32[]{:S(2)}, u32[]{:S(2)}) collective-permute-start(f32[5,24,128]{2,1,0:T(8,128)S(1)} %get-tuple-element.7.own_left_ref), channel_id=1, source_target_pairs={{0,7},{1,0},{2,1},{3,2},{4,3},{5,4},{6,5},{7,6},{8,15},{9,8},{10,9... | collective-permute-start | bytes 184328 | tf_op jit(solution)/shard_map/ppermute | solution.py:325
  35.3 1.2 %collective-permute-start.2 = (f32[5,24,128]{2,1,0:T(8,128)S(1)}, f32[5,24,128]{2,1,0:T(8,128)S(1)}, u32[]{:S(2)}, u32[]{:S(2)}) collective-permute-start(f32[5,24,128]{2,1,0:T(8,128)S(1)} %get-tuple-element.8.own_right_ref), channel_id=1, source_target_pairs={{0,1},{1,2},{2,3},{3,4},{4,5},{5,6},{6,7},{7,0},{8,9},{9,10},{10,1... | collective-permute-start | bytes 184328 | tf_op jit(solution)/shard_map/ppermute | solution.py:325
  36.5 0.1 add_convert_fusion.inside_ref
  36.6 1.8 %collective-permute-done.3.got_right_ref = f32[5,24,128]{2,1,0:T(8,128)S(1)} collective-permute-done((f32[5,24,128]{2,1,0:T(8,128)S(1)}, f32[5,24,128]{2,1,0:T(8,128)S(1)}, u32[]{:S(2)}, u32[]{:S(2)}) %collective-permute-start.3) | collective-permute-done | bytes 61472 | tf_op jit(solution)/shard_map/ppermute | solution.py:325
  38.4 0.0 collective-permute-done.2.got_left_ref
  38.4 5.1 %register.1 = f32[3,32,16,128]{3,2,1,0:T(8,128)} custom-call(f32[36]{0:T(128)S(1)} %reshape.6.tissue_ref, f32[2]{0:T(128)S(1)} %add_convert_fusion.inside_ref, f32[32,24,128]{2,1,0:T(8,128)S(1)} %all-to-all-done.moving_ref, f32[32,16,128]{2,1,0:T(8,128)S(1)} %copy-done.1, f32[3,32,16,128]{3,2,1,0:T(8,128)S(1)} %copy-done, ...), custom_call_target="tpu_custom_call" | custom-call | tf_op jit(solution)/shard_map/register/pallas_call | solution.py:303
Async XLA Ops:
  0.0 13.8 %copy-start = (f32[3,32,16,128]{3,2,1,0:T(8,128)S(1)}, f32[3,32,16,128]{3,2,1,0:T(8,128)}, u32[]{:S(2)}) copy-start(f32[3,32,16,128]{3,2,1,0:T(8,128)} %field_ref.3) | copy-start | bytes 2359300
  0.0 1.0 %copy-start.2 = (f32[1,512,128]{2,1,0:T(8,128)S(1)}, f32[1,512,128]{2,1,0:T(8,128)}, u32[]{:S(2)}) copy-start(f32[1,512,128]{2,1,0:T(8,128)} %param.4) | copy-start | bytes 786436
  1.8 12.0 %copy-start.1 = (f32[32,16,128]{2,1,0:T(8,128)S(1)}, f32[32,16,128]{2,1,0:T(8,128)}, u32[]{:S(2)}) copy-start(f32[32,16,128]{2,1,0:T(8,128)} %fixed_ref.3) | copy-start | bytes 786436
  1.8 31.6 %all-to-all-start = ((f32[32,24,128]{2,1,0:T(8,128)}), f32[32,24,128]{2,1,0:T(8,128)S(1)}, u32[]{:S(2)}, u32[]{:S(2)}) async-start(f32[32,24,128]{2,1,0:T(8,128)} %cut.1), calls=%async_computation | async-start | bytes 786432 | tf_op jit(solution)/shard_map/all_to_all | solution.py:332
  13.9 4.7 %copy-start.3 = (s32[4,32,8]{1,2,0:T(8,128)S(1)}, s32[4,32,8]{1,2,0:T(8,128)}, u32[]{:S(2)}) copy-start(s32[4,32,8]{1,2,0:T(8,128)} %param.7) | copy-start | bytes 12292
  13.9 13.9 %collective-permute-start = (f32[4,32,4,128]{3,2,1,0:T(4,128)S(1)}, f32[4,32,4,128]{3,2,1,0:T(4,128)S(1)}, u32[]{:S(2)}, u32[]{:S(2)}) collective-permute-start(f32[4,32,4,128]{3,2,1,0:T(4,128)S(1)} %get-tuple-element.9), channel_id=1, source_target_pairs={{0,248},{8,0},{16,8},{24,16},{32,24},{40,32},{48,40},{56,48},{64,5... | collective-permute-start | bytes 786440 | tf_op jit(solution)/shard_map/ppermute | solution.py:325
  18.7 14.6 %collective-permute-start.1 = (f32[4,32,4,128]{3,2,1,0:T(4,128)S(1)}, f32[4,32,4,128]{3,2,1,0:T(4,128)S(1)}, u32[]{:S(2)}, u32[]{:S(2)}) collective-permute-start(f32[4,32,4,128]{3,2,1,0:T(4,128)S(1)} %get-tuple-element.10), channel_id=1, source_target_pairs={{0,8},{8,16},{16,24},{24,32},{32,40},{40,48},{48,56},{56,64},{64,7... | collective-permute-start | bytes 786440 | tf_op jit(solution)/shard_map/ppermute | solution.py:325
  34.4 4.1 %collective-permute-start.3 = (f32[5,24,128]{2,1,0:T(8,128)S(1)}, f32[5,24,128]{2,1,0:T(8,128)S(1)}, u32[]{:S(2)}, u32[]{:S(2)}) collective-permute-start(f32[5,24,128]{2,1,0:T(8,128)S(1)} %get-tuple-element.7.own_left_ref), channel_id=1, source_target_pairs={{0,7},{1,0},{2,1},{3,2},{4,3},{5,4},{6,5},{7,6},{8,15},{9,8},{10,9... | collective-permute-start | bytes 184328 | tf_op jit(solution)/shard_map/ppermute | solution.py:325
  35.3 3.1 %collective-permute-start.2 = (f32[5,24,128]{2,1,0:T(8,128)S(1)}, f32[5,24,128]{2,1,0:T(8,128)S(1)}, u32[]{:S(2)}, u32[]{:S(2)}) collective-permute-start(f32[5,24,128]{2,1,0:T(8,128)S(1)} %get-tuple-element.8.own_right_ref), channel_id=1, source_target_pairs={{0,1},{1,2},{2,3},{3,4},{4,5},{5,6},{6,7},{7,0},{8,9},{9,10},{10,1... | collective-permute-start | bytes 184328 | tf_op jit(solution)/shard_map/ppermute | solution.py:325

commit v3 on v2

--- a/solution.py
+++ b/solution.py
@@ -48,40 +48,57 @@
     )(slab.reshape(count, BY, LX))
 
 
-def pack_kernel(moving_ref, fixed_ref, field_ref, halo_ref, left_ref, right_ref):
+def halo_rows(after_ref, before_ref, which, z):
+    return [after_ref[which, z], before_ref[which, z]]
+
+
+def pack_rows(rows, left_ref, right_ref, which):
     group = iota((RY, LX), 1) // EX
-
-    def rows(which, z):
-        if which == 4:
-            return moving_ref[z]
-        core = fixed_ref[z] if which == 3 else field_ref[which, z]
-        return jnp.concatenate([core, halo_ref[which, z]], axis=0)
-
-    for which in range(5):
-
-        def step(z, packs):
-            left, right = packs
-            turned = pltpu.roll(rows(which, z), 4 * z + 4, 1)
-            right = jnp.where(group == z, turned, right)
-            left = jnp.where(group == lax.rem(z + 1, NZ), turned, left)
-            return left, right
-
-        zero = jnp.zeros((RY, LX), f32)
-        left, right = lax.fori_loop(0, NZ, step, (zero, zero), unroll=NZ)
-        left_ref[which] = pltpu.roll(left, LX - EX, 1)
-        right_ref[which] = right
-
-
-def pack(moving, fixed, field, halo):
+    left = right = jnp.zeros((RY, LX), f32)
+    for z in range(NZ):
+        turned = pltpu.roll(rows(z), (EX * (z + 1)) % LX, 1)
+        right = jnp.where(group == z, turned, right)
+        left = jnp.where(group == (z + 1) % NZ, turned, left)
+    left_ref[which] = pltpu.roll(left, LX - EX, 1)
+    right_ref[which] = right
+
+
+def pack_state_kernel(fixed_ref, field_ref, after_ref, before_ref, left_ref, right_ref):
+    for which in range(4):
+
+        def rows(z):
+            core = fixed_ref[z] if which == 3 else field_ref[which, z]
+            return jnp.concatenate([core] + halo_rows(after_ref, before_ref, which, z), axis=0)
+
+        pack_rows(rows, left_ref, right_ref, which)
+
+
+def pack_moving_kernel(moving_ref, left_in_ref, right_in_ref, left_ref, right_ref):
+    del left_in_ref, right_in_ref
+    pack_rows(lambda z: moving_ref[z], left_ref, right_ref, 4)
+
+
+def pack(moving, fixed, field, after, before):
     shape = jax.ShapeDtypeStruct((5, RY, LX), f32)
+    vmem = pl.BlockSpec(memory_space=VMEM)
+    packs = pl.pallas_call(
+        pack_state_kernel,
+        out_shape=(shape, shape),
+        in_specs=[vmem] * 4,
+        out_specs=(vmem, vmem),
+        compiler_params=pltpu.CompilerParams(vmem_limit_bytes=8 * 2**20),
+        cost_estimate=pl.CostEstimate(flops=20000000000, bytes_accessed=2**20, transcendentals=0),
+        name="pack_state",
+    )(fixed, field, after, before)
     return pl.pallas_call(
-        pack_kernel,
+        pack_moving_kernel,
         out_shape=(shape, shape),
-        in_specs=[pl.BlockSpec(memory_space=VMEM)] * 4,
-        out_specs=(pl.BlockSpec(memory_space=VMEM),) * 2,
-        compiler_params=pltpu.CompilerParams(vmem_limit_bytes=8 * 2**20),
-        name="pack",
-    )(moving, fixed, field, halo)
+        in_specs=[vmem] * 3,
+        out_specs=(vmem, vmem),
+        input_output_aliases={1: 0, 2: 1},
+        compiler_params=pltpu.CompilerParams(vmem_limit_bytes=4 * 2**20),
+        name="pack_moving",
+    )(moving, *packs)
 
 
 def recip(x):
@@ -135,7 +152,8 @@
     moving_ref,
     fixed_ref,
     field_ref,
-    halo_ref,
+    after_ref,
+    before_ref,
     own_left_ref,
     own_right_ref,
     got_left_ref,
@@ -241,9 +259,11 @@
             0.5 * (after - before),
         ]
         energy = s[0] * s[0] + s[1] * s[1] + s[2] * s[2] + 0.5
-        gap = jnp.concatenate([fixed_ref[z], halo_ref[3, z]], axis=0) - m
+        gap = jnp.concatenate([fixed_ref[z]] + halo_rows(after_ref, before_ref, 3, z), axis=0) - m
         t = tissue_rows_ref[z // ZG]
-        field = [t * jnp.concatenate([field_ref[c, z], halo_ref[c, z]], axis=0) for c in range(3)]
+        field = [
+            t * jnp.concatenate([field_ref[c, z]] + halo_rows(after_ref, before_ref, c, z), axis=0) for c in range(3)
+        ]
         pulled = attract(field, s, gap, energy, t)
         for c in range(3):
             slope_ref[c, z] = s[c]
@@ -297,13 +317,13 @@
             lax.fori_loop(0, NZ, final, 0, unroll=NZ)
 
 
-def register(tissue, inside, moving, fixed, field, halo, own_left, own_right, got_left, got_right):
+def register(tissue, inside, moving, fixed, field, after, before, own_left, own_right, got_left, got_right):
     smem = pl.BlockSpec(memory_space=pltpu.SMEM)
     vmem = pl.BlockSpec(memory_space=VMEM)
     return pl.pallas_call(
         main_kernel,
         out_shape=jax.ShapeDtypeStruct((3, NZ, BY, LX), f32),
-        in_specs=[smem, smem] + [vmem] * 8,
+        in_specs=[smem, smem] + [vmem] * 9,
         out_specs=vmem,
         scratch_shapes=[
             VMEM((3, NZ, RY, LX), f32),
@@ -317,7 +337,7 @@
         ],
         compiler_params=pltpu.CompilerParams(vmem_limit_bytes=16 * 2**20),
         name="register",
-    )(tissue, inside, moving, fixed, field, halo, own_left, own_right, got_left, got_right)
+    )(tissue, inside, moving, fixed, field, after, before, own_left, own_right, got_left, got_right)
 
 
 def turn(x, axis, by):
@@ -334,17 +354,16 @@
     state = jnp.concatenate([start_field, fixed_image[None]], axis=0)
     after = turn(state[:, :, 0 : HY // 2], "row", -1)
     before = turn(state[:, :, BY - HY // 2 :], "row", 1)
-    halo = jnp.concatenate([after, before], axis=2)
 
     padded = jnp.pad(tissue_mask, ((0, 0), (1, 1), (1, 1))).astype(f32)
     tissue = lax.dynamic_slice(padded, (0, row, col), (NZ // ZG, 3, 3)).reshape(-1)
     inside = jnp.stack([col > 0, col < lax.axis_size("col") - 1]).astype(f32)
 
-    own_left, own_right = pack(moving, fixed_image, start_field, halo)
+    own_left, own_right = pack(moving, fixed_image, start_field, after, before)
     got_left = turn(own_right, "col", 1)
     got_right = turn(own_left, "col", -1)
     return register(
-        tissue, inside, moving, fixed_image, start_field, halo, own_left, own_right, got_left, got_right
+        tissue, inside, moving, fixed_image, start_field, after, before, own_left, own_right, got_left, got_right
     )
 
 

time: 44.4 us -> 41.6 us (0.937); the launches traced: 43.5 us -> 41.3 us
  waiting for transfers between devices: 16.1 us -> 13 us
  other arithmetic: 0.37 us -> 1.54 us
    ppermute x4, waiting for transfers between devices: 16.1 us -> 1.83 us  [turn(): return lax.ppermute(x, axis, [(i, (i + by) % size) for i in range(size)])]
    all_to_all x1, waiting for transfers between devices: 0.01 us -> 11.2 us  [body(): lax.all_to_all(blocks, 'row', split_axis=0, concat_axis=0, tiled=True)]
    all_to_all x1, starting transfers between devices: 12 us -> 5.63 us  [body(): lax.all_to_all(blocks, 'row', split_axis=0, concat_axis=0, tiled=True)]
    ppermute x4, starting transfers between devices: 6.88 us -> 13.2 us  [turn(): return lax.ppermute(x, axis, [(i, (i + by) % size) for i in range(size)])]
    concatenate x1, other arithmetic: 0.11 us -> 1.38 us  [body(): state = jnp.concatenate([start_field, fixed_image[None]], axis=0)]
    pallas_call x1 -> x2, Pallas kernels: 0.97 us -> 1.01 us  [the longest x1 0.78 us: pack(): pl.pallas_call(pack_state_kernel, out_shape=(shape, shape), in_specs=[vme...]
  transfers between devices with their start and end apart: 5 -> 5, of which waited for: 3 -> 2; matrix products, arithmetic and copies ran while one was open for 1% -> 1% of each run, Pallas kernels for 0% -> 4%
where the time goes in v3:
time: 41.6 us; the launch traced here: 41.3 us
  starting transfers between devices  18.9 us (45%)
  waiting for transfers between devices  13 us (31%)
  Pallas kernels  6.89 us (17%)
  other arithmetic  1.54 us (4%)
  local copies, waits for them, and re-layouts  0.92 us (2%)
    ppermute x4, starting transfers between devices, turn(): return lax.ppermute(x, axis, [(i, (i + by) % size) for i in range(size)])  13.2 us
    all_to_all x1, waiting for transfers between devices, body(): lax.all_to_all(blocks, 'row', split_axis=0, concat_axis=0, tiled=True)  11.2 us
    all_to_all x1, starting transfers between devices, body(): lax.all_to_all(blocks, 'row', split_axis=0, concat_axis=0, tiled=True)  5.63 us
    pallas_call x1, Pallas kernels, register(): pl.pallas_call(main_kernel, out_shape=jax.ShapeDtypeStruct((3, NZ, BY, LX...  5.1 us
    ppermute x4, waiting for transfers between devices, turn(): return lax.ppermute(x, axis, [(i, (i + by) % size) for i in range(size)])  1.83 us
    concatenate x1, other arithmetic, body(): state = jnp.concatenate([start_field, fixed_image[None]], axis=0)  1.38 us
  transfers between devices with their start and end apart: 5, of which 2 were waited for; matrix products, arithmetic and copies ran while one was open for 1% of the time, Pallas kernels for 4%

profile of v3, /device:TPU:1, one launch (start us, length us, event | category | flops | bytes accessed | tf_op | source)
XLA Modules:
  0.0 41.3 jit_solution(4180609969797944802)
XLA Ops:
  0.0 0.0 copy-start.2
  0.0 1.4 %pad_maximum_fusion = (f32[4,32,4,128]{3,2,1,0:T(4,128)S(1)}, f32[4,32,4,128]{3,2,1,0:T(4,128)S(1)}) fusion(f32[1,32,16,128]{3,2,1,0:T(8,128)} %bitcast.4, f32[3,32,16,128]{3,2,1,0:T(8,128)} %field_ref.3), kind=kLoop, calls=%fused_computation | loop fusion | flops 131072 | bytes 1572864 | tf_op jit(solution)/shard_map/concatenate | solution.py:354
  1.4 0.0 copy-start
  1.4 2.1 %collective-permute-start.1 = (f32[4,32,4,128]{3,2,1,0:T(4,128)S(1)}, f32[4,32,4,128]{3,2,1,0:T(4,128)S(1)}, u32[]{:S(2)}, u32[]{:S(2)}) collective-permute-start(f32[4,32,4,128]{3,2,1,0:T(4,128)S(1)} %get-tuple-element.13), channel_id=1, source_target_pairs={{0,8},{8,16},{16,24},{24,32},{32,40},{40,48},{48,56},{56,64},{64,7... | collective-permute-start | bytes 786440 | tf_op jit(solution)/shard_map/ppermute | solution.py:345
  3.5 6.6 %collective-permute-start = (f32[4,32,4,128]{3,2,1,0:T(4,128)S(1)}, f32[4,32,4,128]{3,2,1,0:T(4,128)S(1)}, u32[]{:S(2)}, u32[]{:S(2)}) collective-permute-start(f32[4,32,4,128]{3,2,1,0:T(4,128)S(1)} %get-tuple-element.14), channel_id=1, source_target_pairs={{0,248},{8,0},{16,8},{24,16},{32,24},{40,32},{48,40},{56,48},{64,5... | collective-permute-start | bytes 786440 | tf_op jit(solution)/shard_map/ppermute | solution.py:345
  10.2 0.0 copy-done.2
  10.2 0.8 %cut.1 = f32[32,24,128]{2,1,0:T(8,128)} custom-call(f32[32,16,128]{2,1,0:T(8,128)S(1)} %bitcast.5), custom_call_target="tpu_custom_call" | custom-call | tf_op jit(solution)/shard_map/cut/pallas_call | solution.py:41
  10.9 0.0 copy-start.1
  10.9 5.6 %all-to-all-start = ((f32[32,24,128]{2,1,0:T(8,128)}), f32[32,24,128]{2,1,0:T(8,128)S(1)}, u32[]{:S(2)}, u32[]{:S(2)}) async-start(f32[32,24,128]{2,1,0:T(8,128)} %cut.1), calls=%async_computation | async-start | bytes 786432 | tf_op jit(solution)/shard_map/all_to_all | solution.py:352
  16.6 0.0 copy-start.3
  16.6 0.7 %copy-done.3 = s32[4,32,8]{1,2,0:T(8,128)S(1)} copy-done((s32[4,32,8]{1,2,0:T(8,128)S(1)}, s32[4,32,8]{1,2,0:T(8,128)}, u32[]{:S(2)}) %copy-start.3) | copy-done | bytes 4120
  17.3 0.1 fusion
  17.4 0.1 copy.8
  17.5 0.1 reshape.6.tissue_ref
  17.6 0.0 collective-permute-done.1.before_ref
  17.6 0.0 collective-permute-done.after_ref
  17.6 0.0 copy-done
  17.6 0.0 copy-done.1
  17.6 0.8 %pack_state.1 = (f32[5,24,128]{2,1,0:T(8,128)S(1)}, f32[5,24,128]{2,1,0:T(8,128)S(1)}) custom-call(f32[32,16,128]{2,1,0:T(8,128)S(1)} %copy-done.1, f32[3,32,16,128]{3,2,1,0:T(8,128)S(1)} %copy-done, f32[4,32,4,128]{3,2,1,0:T(4,128)S(1)} %collective-permute-done.after_ref, f32[4,32,4,128]{3,2,1,0:T(4,128)S(1)} %collective-permute-done.1.before_ref), custom_call_target="tpu_custom_call" | custom-call | flops 20000000000 | bytes 1048576 | tf_op jit(solution)/shard_map/pack_state/pallas_call | solution.py:84
  18.4 11.2 %all-to-all-done.moving_ref = f32[32,24,128]{2,1,0:T(8,128)S(1)} async-done(((f32[32,24,128]{2,1,0:T(8,128)}), f32[32,24,128]{2,1,0:T(8,128)S(1)}, u32[]{:S(2)}, u32[]{:S(2)}) %all-to-all-start) | async-done | bytes 393248 | tf_op jit(solution)/shard_map/all_to_all | solution.py:352
  29.6 0.2 pack_moving.1
  29.9 3.3 %collective-permute-start.3 = (f32[5,24,128]{2,1,0:T(8,128)S(1)}, f32[5,24,128]{2,1,0:T(8,128)S(1)}, u32[]{:S(2)}, u32[]{:S(2)}) collective-permute-start(f32[5,24,128]{2,1,0:T(8,128)S(1)} %get-tuple-element.11.own_left_ref), channel_id=1, source_target_pairs={{0,7},{1,0},{2,1},{3,2},{4,3},{5,4},{6,5},{7,6},{8,15},{9,8},{10,9... | collective-permute-start | bytes 184328 | tf_op jit(solution)/shard_map/ppermute | solution.py:345
  33.1 1.2 %collective-permute-start.2 = (f32[5,24,128]{2,1,0:T(8,128)S(1)}, f32[5,24,128]{2,1,0:T(8,128)S(1)}, u32[]{:S(2)}, u32[]{:S(2)}) collective-permute-start(f32[5,24,128]{2,1,0:T(8,128)S(1)} %get-tuple-element.12.own_right_ref), channel_id=1, source_target_pairs={{0,1},{1,2},{2,3},{3,4},{4,5},{5,6},{6,7},{7,0},{8,9},{9,10},{10,1... | collective-permute-start | bytes 184328 | tf_op jit(solution)/shard_map/ppermute | solution.py:345
  34.3 0.1 add_convert_fusion.inside_ref
  34.4 1.8 %collective-permute-done.3.got_right_ref = f32[5,24,128]{2,1,0:T(8,128)S(1)} collective-permute-done((f32[5,24,128]{2,1,0:T(8,128)S(1)}, f32[5,24,128]{2,1,0:T(8,128)S(1)}, u32[]{:S(2)}, u32[]{:S(2)}) %collective-permute-start.3) | collective-permute-done | bytes 61472 | tf_op jit(solution)/shard_map/ppermute | solution.py:345
  36.2 0.0 collective-permute-done.2.got_left_ref
  36.2 5.1 %register.1 = f32[3,32,16,128]{3,2,1,0:T(8,128)} custom-call(f32[36]{0:T(128)S(1)} %reshape.6.tissue_ref, f32[2]{0:T(128)S(1)} %add_convert_fusion.inside_ref, f32[32,24,128]{2,1,0:T(8,128)S(1)} %all-to-all-done.moving_ref, f32[32,16,128]{2,1,0:T(8,128)S(1)} %copy-done.1, f32[3,32,16,128]{3,2,1,0:T(8,128)S(1)} %copy-done, ...), custom_call_target="tpu_custom_call" | custom-call | tf_op jit(solution)/shard_map/register/pallas_call | solution.py:323
Async XLA Ops:
  0.0 10.2 %copy-start.2 = (f32[1,512,128]{2,1,0:T(8,128)S(1)}, f32[1,512,128]{2,1,0:T(8,128)}, u32[]{:S(2)}) copy-start(f32[1,512,128]{2,1,0:T(8,128)} %param.4) | copy-start | bytes 786436
  1.4 16.2 %copy-start = (f32[3,32,16,128]{3,2,1,0:T(8,128)S(1)}, f32[3,32,16,128]{3,2,1,0:T(8,128)}, u32[]{:S(2)}) copy-start(f32[3,32,16,128]{3,2,1,0:T(8,128)} %field_ref.3) | copy-start | bytes 2359300
  1.4 16.2 %collective-permute-start.1 = (f32[4,32,4,128]{3,2,1,0:T(4,128)S(1)}, f32[4,32,4,128]{3,2,1,0:T(4,128)S(1)}, u32[]{:S(2)}, u32[]{:S(2)}) collective-permute-start(f32[4,32,4,128]{3,2,1,0:T(4,128)S(1)} %get-tuple-element.13), channel_id=1, source_target_pairs={{0,8},{8,16},{16,24},{24,32},{32,40},{40,48},{48,56},{56,64},{64,7... | collective-permute-start | bytes 786440 | tf_op jit(solution)/shard_map/ppermute | solution.py:345
  3.5 14.1 %collective-permute-start = (f32[4,32,4,128]{3,2,1,0:T(4,128)S(1)}, f32[4,32,4,128]{3,2,1,0:T(4,128)S(1)}, u32[]{:S(2)}, u32[]{:S(2)}) collective-permute-start(f32[4,32,4,128]{3,2,1,0:T(4,128)S(1)} %get-tuple-element.14), channel_id=1, source_target_pairs={{0,248},{8,0},{16,8},{24,16},{32,24},{40,32},{48,40},{56,48},{64,5... | collective-permute-start | bytes 786440 | tf_op jit(solution)/shard_map/ppermute | solution.py:345
  10.9 6.7 %copy-start.1 = (f32[32,16,128]{2,1,0:T(8,128)S(1)}, f32[32,16,128]{2,1,0:T(8,128)}, u32[]{:S(2)}) copy-start(f32[32,16,128]{2,1,0:T(8,128)} %fixed_ref.3) | copy-start | bytes 786436
  10.9 18.7 %all-to-all-start = ((f32[32,24,128]{2,1,0:T(8,128)}), f32[32,24,128]{2,1,0:T(8,128)S(1)}, u32[]{:S(2)}, u32[]{:S(2)}) async-start(f32[32,24,128]{2,1,0:T(8,128)} %cut.1), calls=%async_computation | async-start | bytes 786432 | tf_op jit(solution)/shard_map/all_to_all | solution.py:352
  16.6 0.7 %copy-start.3 = (s32[4,32,8]{1,2,0:T(8,128)S(1)}, s32[4,32,8]{1,2,0:T(8,128)}, u32[]{:S(2)}) copy-start(s32[4,32,8]{1,2,0:T(8,128)} %param.7) | copy-start | bytes 12292
  29.9 6.4 %collective-permute-start.3 = (f32[5,24,128]{2,1,0:T(8,128)S(1)}, f32[5,24,128]{2,1,0:T(8,128)S(1)}, u32[]{:S(2)}, u32[]{:S(2)}) collective-permute-start(f32[5,24,128]{2,1,0:T(8,128)S(1)} %get-tuple-element.11.own_left_ref), channel_id=1, source_target_pairs={{0,7},{1,0},{2,1},{3,2},{4,3},{5,4},{6,5},{7,6},{8,15},{9,8},{10,9... | collective-permute-start | bytes 184328 | tf_op jit(solution)/shard_map/ppermute | solution.py:345
  33.1 3.1 %collective-permute-start.2 = (f32[5,24,128]{2,1,0:T(8,128)S(1)}, f32[5,24,128]{2,1,0:T(8,128)S(1)}, u32[]{:S(2)}, u32[]{:S(2)}) collective-permute-start(f32[5,24,128]{2,1,0:T(8,128)S(1)} %get-tuple-element.12.own_right_ref), channel_id=1, source_target_pairs={{0,1},{1,2},{2,3},{3,4},{4,5},{5,6},{6,7},{7,0},{8,9},{9,10},{10,1... | collective-permute-start | bytes 184328 | tf_op jit(solution)/shard_map/ppermute | solution.py:345

commit v4 on v0

v4 whole, which is shorter than its diff:
```python
import jax
import jax.numpy as jnp
from jax import lax
from jax.experimental import pallas as pl
from jax.experimental.pallas import tpu as pltpu
from jax.sharding import PartitionSpec as P

ITERS = 3
pull_rate = 1.0
smooth_rate = 0.16

NZ = 32
BY = 16
HY = 8
RY = BY + HY
LX = 128
EX = LX // NZ
ZG = 8
GROUPS = NZ // ZG

VMEM = pltpu.VMEM
f32 = jnp.float32
vmem = pl.BlockSpec(memory_space=VMEM)
smem = pl.BlockSpec(memory_space=pltpu.SMEM)


def params(mib):
    return pltpu.CompilerParams(vmem_limit_bytes=mib * 2**20)


def iota(shape, dim):
    return lax.broadcasted_iota(jnp.int32, shape, dim)


def cut_kernel(slab_ref, out_ref):
    count = slab_ref.shape[0]
    low = iota((HY, LX), 0) < HY // 2
    zero = jnp.zeros((HY, LX), f32)
    for i in range(count):
        after = slab_ref[i + 1, 0:HY] if i + 1 < count else zero
        before = slab_ref[i - 1, HY:BY] if i else zero
        out_ref[i, 0:BY] = slab_ref[i]
        out_ref[i, BY:RY] = jnp.where(low, after, before)


def cut(slab):
    count = slab.shape[1] // BY
    return pl.pallas_call(
        cut_kernel,
        out_shape=jax.ShapeDtypeStruct((count, RY, LX), f32),
        in_specs=[vmem],
        out_specs=vmem,
        compiler_params=params(4),
        name="cut",
    )(slab.reshape(count, BY, LX))


def ring(core, after, before):
    return jnp.concatenate([core, after, before], axis=0)


def pack_rows(rows, refs, which):
    group = iota((RY, LX), 1) // EX
    packs = [jnp.zeros((RY, LX), f32)] * 4
    offsets = (1, 2, 0, -1)
    for z in range(NZ):
        turned = pltpu.roll(rows(z), (EX * (z + 1)) % LX, 1)
        packs = [jnp.where(group == (z + at) % NZ, turned, p) for at, p in zip(offsets, packs)]
    for at, p, ref in zip(offsets, packs, refs):
        ref[which] = pltpu.roll(p, (-EX * at) % LX, 1) if at else p


def pack_state_kernel(fixed_ref, field_ref, after_ref, before_ref, *refs):
    for which in range(4):

        def rows(z):
            core = fixed_ref[z] if which == 3 else field_ref[which, z]
            return ring(core, after_ref[which, z], before_ref[which, z])

        pack_rows(rows, refs, which)


def pack_moving_kernel(moving_ref, *refs):
    pack_rows(lambda z: moving_ref[z], refs[-4:], 4)


def pack(moving, fixed, field, after, before):
    shapes = (jax.ShapeDtypeStruct((5, RY, LX), f32),) * 4
    packs = pl.pallas_call(
        pack_state_kernel,
        out_shape=shapes,
        in_specs=[vmem] * 4,
        out_specs=(vmem,) * 4,
        compiler_params=params(8),
        cost_estimate=pl.CostEstimate(flops=20000000000, bytes_accessed=2**20, transcendentals=0),
        name="pack_state",
    )(fixed, field, after, before)
    return pl.pallas_call(
        pack_moving_kernel,
        out_shape=shapes,
        in_specs=[vmem] * 5,
        out_specs=(vmem,) * 4,
        input_output_aliases={1: 0, 2: 1, 3: 2, 4: 3},
        compiler_params=params(4),
        name="pack_moving",
    )(moving, *packs)


def recip(x):
    r = pl.reciprocal(x, approx=True)
    return r * (2.0 - x * r)


def energy_of(s):
    return s[0] * s[0] + s[1] * s[1] + s[2] * s[2] + 0.5


def attract(field, slopes, gap, energy, tissue):
    residual = gap - (slopes[0] * field[0] + slopes[1] * field[1] + slopes[2] * field[2])
    rate = pull_rate * tissue * residual * recip(energy + residual * residual)
    return [field[c] + rate * slopes[c] for c in range(3)]


def tissue_rows(tissue_ref, column, group):
    row = iota((RY, LX), 0)

    def at(k):
        return tissue_ref[(group * 3 + k) * 3 + column]

    return jnp.where(row < BY, at(1), jnp.where(row < BY + HY // 2, at(2), at(0)))


def core_kernel(
    tissue_ref,
    moving_ref,
    fixed_ref,
    field_ref,
    after_ref,
    before_ref,
    out_ref,
    slope_ref,
    energy_ref,
    gap_ref,
    ping_ref,
    pong_ref,
    spread_ref,
    keep_ref,
):
    top, end = HY, HY + RY
    zero = jnp.zeros((RY, LX), f32)
    cells = [tissue_rows(tissue_ref, 1, g) for g in range(GROUPS)]
    for g in range(GROUPS):
        own = cells[g]
        spread = smooth_rate * own
        spread_ref[g] = spread
        flat = 2.0 * own + pltpu.roll(own, 1, 0) + pltpu.roll(own, RY - 1, 0)
        below = cells[g - 1] if g else zero
        above = cells[g + 1] if g + 1 < GROUPS else zero
        keep_ref[3 * g] = 1.0 - spread * (flat + below + own)
        keep_ref[3 * g + 1] = 1.0 - spread * (flat + own + own)
        keep_ref[3 * g + 2] = 1.0 - spread * (flat + own + above)
    for ref in (ping_ref, pong_ref):
        for c in range(3):
            ref[c, 0, top:end] = zero
            ref[c, NZ + 1, top:end] = zero

    def put(ref, z, pulled):
        for c in range(3):
            ref[c, z + 1, top:end] = pulled[c]
            ref[c, z + 1, 0:top] = pulled[c][BY:]
            ref[c, z + 1, end : end + HY] = pulled[c][:HY]

    for z in range(NZ):
        m = moving_ref[z]
        above = moving_ref[z + 1] if z < NZ - 1 else zero
        below = moving_ref[z - 1] if z else zero
        s = [
            0.5 * (above - below),
            0.5 * (pltpu.roll(m, RY - 1, 0) - pltpu.roll(m, 1, 0)),
            0.5 * (pltpu.roll(m, LX - 1, 1) - pltpu.roll(m, 1, 1)),
        ]
        energy = energy_of(s)
        gap = ring(fixed_ref[z], after_ref[3, z], before_ref[3, z]) - m
        t = cells[z // ZG]
        field = [t * ring(field_ref[c, z], after_ref[c, z], before_ref[c, z]) for c in range(3)]
        put(ping_ref, z, attract(field, s, gap, energy, t))
        for c in range(3):
            slope_ref[c, z] = s[c]
        energy_ref[z] = energy
        gap_ref[z] = gap

    def smoothed(src, z, c, rows):
        def at(dz, dy):
            return src[c, z + 1 + dz, top + dy : top + dy + rows]

        p = at(0, 0)
        around = (
            (at(1, 0) + at(-1, 0)) + (at(0, 1) + at(0, -1)) + (pltpu.roll(p, 1, 1) + pltpu.roll(p, LX - 1, 1))
        )
        g, k = z // ZG, z % ZG
        keep = keep_ref[3 * g + (0 if k == 0 else 2 if k == ZG - 1 else 1), 0:rows]
        return keep * p + spread_ref[g, 0:rows] * around

    src, dst = ping_ref, pong_ref
    for sweep in range(ITERS - 1):
        for z in range(NZ):
            field = [smoothed(src, z, c, RY) for c in range(3)]
            s = [slope_ref[c, z] for c in range(3)]
            put(dst, z, attract(field, s, gap_ref[z], energy_ref[z], cells[z // ZG]))
        src, dst = dst, src
    for z in range(NZ):
        for c in range(3):
            out_ref[c, z] = smoothed(src, z, c, BY)


def core(tissue, moving, fixed, field, after, before):
    return pl.pallas_call(
        core_kernel,
        out_shape=jax.ShapeDtypeStruct((3, NZ, BY, LX), f32),
        in_specs=[smem] + [vmem] * 5,
        out_specs=vmem,
        scratch_shapes=[
            VMEM((3, NZ, RY, LX), f32),
            VMEM((NZ, RY, LX), f32),
            VMEM((NZ, RY, LX), f32),
            VMEM((3, NZ + 2, RY + 2 * HY, LX), f32),
            VMEM((3, NZ + 2, RY + 2 * HY, LX), f32),
            VMEM((GROUPS, RY, LX), f32),
            VMEM((3 * GROUPS, RY, LX), f32),
        ],
        compiler_params=params(16),
        cost_estimate=pl.CostEstimate(flops=10000000000, bytes_accessed=2**20, transcendentals=0),
        name="core",
    )(tissue, moving, fixed, field, after, before)


def chain_neighbours(chain):
    lane = iota((RY, LX), 1)
    j = lane % EX
    first, last = j == 0, j == EX - 1
    low, high = lane < EX, lane >= LX - EX
    above = [pltpu.roll(p, LX - EX, 1) for p in chain]
    below = [pltpu.roll(p, EX, 1) for p in chain]
    out = []
    for k, p in enumerate(chain):
        before = jnp.where(last, above[k - 1], p) if k else p
        after = jnp.where(first, below[k + 1], p) if k + 1 < len(chain) else p
        out.append(
            (
                jnp.where(high, 0.0, above[k]),
                jnp.where(low, 0.0, below[k]),
                pltpu.roll(p, RY - 1, 0),
                pltpu.roll(p, 1, 0),
                pltpu.roll(after, LX - 1, 1),
                pltpu.roll(before, 1, 1),
            )
        )
    return out


def total(neighbours):
    above, below, after_y, before_y, after_x, before_x = neighbours
    return ((above + below) + (after_y + before_y)) + (after_x + before_x)


def edge_kernel(
    tissue_ref,
    inside_ref,
    left_ref,
    left_in_ref,
    right_ref,
    right_in_ref,
    got_left_ref,
    got_right_ref,
    core_ref,
    out_ref,
):
    lane = iota((RY, LX), 1)

    def side(refs, columns, outer, inside):
        tissue = []
        for column in columns:
            cell = tissue_rows(tissue_ref, column, GROUPS - 1)
            for g in range(GROUPS - 2, -1, -1):
                cell = jnp.where(lane < (g + 1) * ZG * EX, tissue_rows(tissue_ref, column, g), cell)
            tissue.append(cell)
        spread = [smooth_rate * t for t in tissue]
        keep = [1.0 - b * total(n) for b, n in zip(spread, chain_neighbours(tissue))]
        moving = [ref[4] * inside if k == outer else ref[4] for k, ref in enumerate(refs)]
        slopes = [
            [0.5 * (n[0] - n[1]), 0.5 * (n[2] - n[3]), 0.5 * (n[4] - n[5])] for n in chain_neighbours(moving)
        ]
        energy = [energy_of(s) for s in slopes]
        gap = [ref[3] - m for ref, m in zip(refs, moving)]
        field = [[t * ref[c] for c in range(3)] for t, ref in zip(tissue, refs)]
        for sweep in range(ITERS):
            pulled = [attract(*x) for x in zip(field, slopes, gap, energy, tissue)]
            near = [chain_neighbours([p[c] for p in pulled]) for c in range(3)]
            field = [
                [keep[k] * pulled[k][c] + spread[k] * total(near[c][k]) for c in range(3)] for k in range(len(refs))
            ]
        return field[1]

    left = side((got_left_ref, left_ref, left_in_ref), (0, 1, 1), 0, inside_ref[0])
    right = side((right_in_ref, right_ref, got_right_ref), (1, 1, 2), 2, inside_ref[1])
    at_left, at_right = lane[:BY] < EX, lane[:BY] >= LX - EX
    for z in range(NZ):
        for c in range(3):
            a = pltpu.roll(left[c][:BY], (-EX * z) % LX, 1)
            b = pltpu.roll(right[c][:BY], (-EX * (z + 1)) % LX, 1)
            out_ref[c, z] = jnp.where(at_left, a, jnp.where(at_right, b, core_ref[c, z]))


def edge(tissue, inside, packs, got_left, got_right, middle):
    return pl.pallas_call(
        edge_kernel,
        out_shape=jax.ShapeDtypeStruct((3, NZ, BY, LX), f32),
        in_specs=[smem, smem] + [vmem] * 7,
        out_specs=vmem,
        compiler_params=params(16),
        name="edge",
    )(tissue, inside, *packs, got_left, got_right, middle)


def turn(x, axis, by):
    size = lax.axis_size(axis)
    return lax.ppermute(x, axis, [(i, (i + by) % size) for i in range(size)])


def body(moving_slab, fixed_image, start_field, tissue_mask):
    row = lax.axis_index("row")
    col = lax.axis_index("col")
    blocks = cut(moving_slab)
    moving = lax.all_to_all(blocks, "row", split_axis=0, concat_axis=0, tiled=True)

    state = jnp.concatenate([start_field, fixed_image[None]], axis=0)
    after = turn(state[:, :, 0 : HY // 2], "row", -1)
    before = turn(state[:, :, BY - HY // 2 :], "row", 1)

    padded = jnp.pad(tissue_mask, ((0, 0), (1, 1), (1, 1))).astype(f32)
    tissue = lax.dynamic_slice(padded, (0, row, col), (GROUPS, 3, 3)).reshape(-1)
    inside = jnp.stack([col > 0, col < lax.axis_size("col") - 1]).astype(f32)

    packs = pack(moving, fixed_image, start_field, after, before)
    left, _, right, _ = packs
    got_left = turn(right, "col", 1)
    got_right = turn(left, "col", -1)
    middle = core(tissue, moving, fixed_image, start_field, after, before)
    return edge(tissue, inside, packs, got_left, got_right, middle)


def solution(mesh):
    in_specs = (P("row", None, "col"), P(None, "row", "col"), P(None, None, "row", "col"), P())
    out_specs = P(None, None, "row", "col")
    return jax.shard_map(body, mesh=mesh, in_specs=in_specs, out_specs=out_specs, check_vma=False)
```

time: 118 us -> 41.2 us (0.35)
  the two profiles are of different devices: /device:TPU:126 before, /device:TPU:1 now
where the time goes in v4:
time: 41.2 us; the launch traced here: 40.9 us
  starting transfers between devices  18.9 us (46%)
  waiting for transfers between devices  11.1 us (27%)
  Pallas kernels  8.38 us (20%)
  other arithmetic  1.54 us (4%)
  local copies, waits for them, and re-layouts  0.92 us (2%)
    ppermute x4, starting transfers between devices, turn(): return lax.ppermute(x, axis, [(i, (i + by) % size) for i in range(size)])  13.2 us
    all_to_all x1, waiting for transfers between devices, body(): lax.all_to_all(blocks, 'row', split_axis=0, concat_axis=0, tiled=True)  11.1 us
    all_to_all x1, starting transfers between devices, body(): lax.all_to_all(blocks, 'row', split_axis=0, concat_axis=0, tiled=True)  5.63 us
    pallas_call x1, Pallas kernels, edge(): pl.pallas_call(edge_kernel, out_shape=jax.ShapeDtypeStruct((3, NZ, BY, LX...  3.58 us
    pallas_call x1, Pallas kernels, core(): pl.pallas_call(core_kernel, out_shape=jax.ShapeDtypeStruct((3, NZ, BY, LX...  2.93 us
    concatenate x1, other arithmetic, body(): state = jnp.concatenate([start_field, fixed_image[None]], axis=0)  1.38 us
    pallas_call x1, Pallas kernels, pack(): pl.pallas_call(pack_state_kernel, out_shape=shapes, in_specs=[vmem] * 4,...  0.87 us
  transfers between devices with their start and end apart: 5, of which 1 were waited for; matrix products, arithmetic and copies ran while one was open for 1% of the time, Pallas kernels for 11%

profile of v4, /device:TPU:1, one launch (start us, length us, event | category | flops | bytes accessed | tf_op | source)
XLA Modules:
  0.0 40.9 jit_solution(2206858792344851002)
XLA Ops:
  0.0 0.0 copy-start.1
  0.0 1.4 %pad_maximum_fusion = (f32[4,32,4,128]{3,2,1,0:T(4,128)S(1)}, f32[4,32,4,128]{3,2,1,0:T(4,128)S(1)}) fusion(f32[1,32,16,128]{3,2,1,0:T(8,128)} %bitcast.5, f32[3,32,16,128]{3,2,1,0:T(8,128)} %field_ref.3), kind=kLoop, calls=%fused_computation | loop fusion | flops 131072 | bytes 1572864 | tf_op jit(solution)/shard_map/concatenate | solution.py:336
  1.4 0.0 copy-start
  1.4 2.1 %collective-permute-start.1 = (f32[4,32,4,128]{3,2,1,0:T(4,128)S(1)}, f32[4,32,4,128]{3,2,1,0:T(4,128)S(1)}, u32[]{:S(2)}, u32[]{:S(2)}) collective-permute-start(f32[4,32,4,128]{3,2,1,0:T(4,128)S(1)} %get-tuple-element.21), channel_id=1, source_target_pairs={{0,8},{8,16},{16,24},{24,32},{32,40},{40,48},{48,56},{56,64},{64,7... | collective-permute-start | bytes 786440 | tf_op jit(solution)/shard_map/ppermute | solution.py:327
  3.5 6.6 %collective-permute-start = (f32[4,32,4,128]{3,2,1,0:T(4,128)S(1)}, f32[4,32,4,128]{3,2,1,0:T(4,128)S(1)}, u32[]{:S(2)}, u32[]{:S(2)}) collective-permute-start(f32[4,32,4,128]{3,2,1,0:T(4,128)S(1)} %get-tuple-element.22), channel_id=1, source_target_pairs={{0,248},{8,0},{16,8},{24,16},{32,24},{40,32},{48,40},{56,48},{64,5... | collective-permute-start | bytes 786440 | tf_op jit(solution)/shard_map/ppermute | solution.py:327
  10.2 0.0 copy-done.1
  10.2 0.8 %cut.1 = f32[32,24,128]{2,1,0:T(8,128)} custom-call(f32[32,16,128]{2,1,0:T(8,128)S(1)} %bitcast.4), custom_call_target="tpu_custom_call" | custom-call | tf_op jit(solution)/shard_map/cut/pallas_call | solution.py:48
  10.9 0.0 copy-start.2
  10.9 5.6 %all-to-all-start = ((f32[32,24,128]{2,1,0:T(8,128)}), f32[32,24,128]{2,1,0:T(8,128)S(1)}, u32[]{:S(2)}, u32[]{:S(2)}) async-start(f32[32,24,128]{2,1,0:T(8,128)} %cut.1), calls=%async_computation | async-start | bytes 786432 | tf_op jit(solution)/shard_map/all_to_all | solution.py:334
  16.6 0.0 copy-start.3
  16.6 0.7 %copy-done.3 = s32[4,32,8]{1,2,0:T(8,128)S(1)} copy-done((s32[4,32,8]{1,2,0:T(8,128)S(1)}, s32[4,32,8]{1,2,0:T(8,128)}, u32[]{:S(2)}) %copy-start.3) | copy-done | bytes 4120
  17.3 0.1 fusion
  17.4 0.1 copy.10
  17.5 0.1 reshape.6.tissue_ref
  17.6 0.1 add_convert_fusion.inside_ref
  17.7 0.0 collective-permute-done.1.before_ref
  17.7 0.0 collective-permute-done.after_ref
  17.7 0.0 copy-done
  17.7 0.0 copy-done.2
  17.7 0.9 %pack_state.1 = (f32[5,24,128]{2,1,0:T(8,128)S(1)}, f32[5,24,128]{2,1,0:T(8,128)S(1)}, f32[5,24,128]{2,1,0:T(8,128)S(1)}, f32[5,24,128]{2,1,0:T(8,128)S(1)}) custom-call(f32[32,16,128]{2,1,0:T(8,128)S(1)} %copy-done.2, f32[3,32,16,128]{3,2,1,0:T(8,128)S(1)} %copy-done, f32[4,32,4,128]{3,2,1,0:T(4,128)S(1)} %collective-permute-done.after_ref, ...), custom_call_target="tpu_custom_call" | custom-call | flops 20000000000 | bytes 1048576 | tf_op jit(solution)/shard_map/pack_state/pallas_call | solution.py:89
  18.6 11.1 %all-to-all-done.moving_ref = f32[32,24,128]{2,1,0:T(8,128)S(1)} async-done(((f32[32,24,128]{2,1,0:T(8,128)}), f32[32,24,128]{2,1,0:T(8,128)S(1)}, u32[]{:S(2)}, u32[]{:S(2)}) %all-to-all-start) | async-done | bytes 393248 | tf_op jit(solution)/shard_map/all_to_all | solution.py:334
  29.6 0.2 pack_moving.1
  29.9 3.3 %collective-permute-start.3 = (f32[5,24,128]{2,1,0:T(8,128)S(1)}, f32[5,24,128]{2,1,0:T(8,128)S(1)}, u32[]{:S(2)}, u32[]{:S(2)}) collective-permute-start(f32[5,24,128]{2,1,0:T(8,128)S(1)} %get-tuple-element.17.left_ref), channel_id=1, source_target_pairs={{0,7},{1,0},{2,1},{3,2},{4,3},{5,4},{6,5},{7,6},{8,15},{9,8},{10,9... | collective-permute-start | bytes 184328 | tf_op jit(solution)/shard_map/ppermute | solution.py:327
  33.1 1.2 %collective-permute-start.2 = (f32[5,24,128]{2,1,0:T(8,128)S(1)}, f32[5,24,128]{2,1,0:T(8,128)S(1)}, u32[]{:S(2)}, u32[]{:S(2)}) collective-permute-start(f32[5,24,128]{2,1,0:T(8,128)S(1)} %get-tuple-element.19.right_ref), channel_id=1, source_target_pairs={{0,1},{1,2},{2,3},{3,4},{4,5},{5,6},{6,7},{7,0},{8,9},{9,10},{10,1... | collective-permute-start | bytes 184328 | tf_op jit(solution)/shard_map/ppermute | solution.py:327
  34.3 2.9 %core.1.core_ref = f32[3,32,16,128]{3,2,1,0:T(8,128)S(1)} custom-call(f32[36]{0:T(128)S(1)} %reshape.6.tissue_ref, f32[32,24,128]{2,1,0:T(8,128)S(1)} %all-to-all-done.moving_ref, f32[32,16,128]{2,1,0:T(8,128)S(1)} %copy-done.2, f32[3,32,16,128]{3,2,1,0:T(8,128)S(1)} %copy-done, f32[4,32,4,128]{3,2,1,0:T(4,128)S(1)} %collective-permute-done.after_ref, ...), custom_call_target="tpu_custom_call" | custom-call | flops 10000000000 | bytes 1048576 | tf_op jit(solution)/shard_map/core/pallas_call | solution.py:217
  37.3 0.0 collective-permute-done.3.got_right_ref
  37.3 0.0 collective-permute-done.2.got_left_ref
  37.3 3.6 %edge.1 = f32[3,32,16,128]{3,2,1,0:T(8,128)} custom-call(f32[36]{0:T(128)S(1)} %reshape.6.tissue_ref, f32[2]{0:T(128)S(1)} %add_convert_fusion.inside_ref, f32[5,24,128]{2,1,0:T(8,128)S(1)} %get-tuple-element.17.left_ref, f32[5,24,128]{2,1,0:T(8,128)S(1)} %get-tuple-element.18.left_in_ref, f32[5,24,128]{2,1,0:T(8,128)S(1)} %get-tuple-element.19.right_ref, ...), custom_call_target="tpu_custom_call" | custom-call | tf_op jit(solution)/shard_map/edge/pallas_call | solution.py:315
Async XLA Ops:
  0.0 10.2 %copy-start.1 = (f32[1,512,128]{2,1,0:T(8,128)S(1)}, f32[1,512,128]{2,1,0:T(8,128)}, u32[]{:S(2)}) copy-start(f32[1,512,128]{2,1,0:T(8,128)} %param.4) | copy-start | bytes 786436
  1.4 16.3 %copy-start = (f32[3,32,16,128]{3,2,1,0:T(8,128)S(1)}, f32[3,32,16,128]{3,2,1,0:T(8,128)}, u32[]{:S(2)}) copy-start(f32[3,32,16,128]{3,2,1,0:T(8,128)} %field_ref.3) | copy-start | bytes 2359300
  1.4 16.3 %collective-permute-start.1 = (f32[4,32,4,128]{3,2,1,0:T(4,128)S(1)}, f32[4,32,4,128]{3,2,1,0:T(4,128)S(1)}, u32[]{:S(2)}, u32[]{:S(2)}) collective-permute-start(f32[4,32,4,128]{3,2,1,0:T(4,128)S(1)} %get-tuple-element.21), channel_id=1, source_target_pairs={{0,8},{8,16},{16,24},{24,32},{32,40},{40,48},{48,56},{56,64},{64,7... | collective-permute-start | bytes 786440 | tf_op jit(solution)/shard_map/ppermute | solution.py:327
  3.5 14.2 %collective-permute-start = (f32[4,32,4,128]{3,2,1,0:T(4,128)S(1)}, f32[4,32,4,128]{3,2,1,0:T(4,128)S(1)}, u32[]{:S(2)}, u32[]{:S(2)}) collective-permute-start(f32[4,32,4,128]{3,2,1,0:T(4,128)S(1)} %get-tuple-element.22), channel_id=1, source_target_pairs={{0,248},{8,0},{16,8},{24,16},{32,24},{40,32},{48,40},{56,48},{64,5... | collective-permute-start | bytes 786440 | tf_op jit(solution)/shard_map/ppermute | solution.py:327
  10.9 6.7 %copy-start.2 = (f32[32,16,128]{2,1,0:T(8,128)S(1)}, f32[32,16,128]{2,1,0:T(8,128)}, u32[]{:S(2)}) copy-start(f32[32,16,128]{2,1,0:T(8,128)} %fixed_ref.3) | copy-start | bytes 786436
  10.9 18.7 %all-to-all-start = ((f32[32,24,128]{2,1,0:T(8,128)}), f32[32,24,128]{2,1,0:T(8,128)S(1)}, u32[]{:S(2)}, u32[]{:S(2)}) async-start(f32[32,24,128]{2,1,0:T(8,128)} %cut.1), calls=%async_computation | async-start | bytes 786432 | tf_op jit(solution)/shard_map/all_to_all | solution.py:334
  16.6 0.7 %copy-start.3 = (s32[4,32,8]{1,2,0:T(8,128)S(1)}, s32[4,32,8]{1,2,0:T(8,128)}, u32[]{:S(2)}) copy-start(s32[4,32,8]{1,2,0:T(8,128)} %param.7) | copy-start | bytes 12292
  29.9 7.4 %collective-permute-start.3 = (f32[5,24,128]{2,1,0:T(8,128)S(1)}, f32[5,24,128]{2,1,0:T(8,128)S(1)}, u32[]{:S(2)}, u32[]{:S(2)}) collective-permute-start(f32[5,24,128]{2,1,0:T(8,128)S(1)} %get-tuple-element.17.left_ref), channel_id=1, source_target_pairs={{0,7},{1,0},{2,1},{3,2},{4,3},{5,4},{6,5},{7,6},{8,15},{9,8},{10,9... | collective-permute-start | bytes 184328 | tf_op jit(solution)/shard_map/ppermute | solution.py:327
  33.1 4.1 %collective-permute-start.2 = (f32[5,24,128]{2,1,0:T(8,128)S(1)}, f32[5,24,128]{2,1,0:T(8,128)S(1)}, u32[]{:S(2)}, u32[]{:S(2)}) collective-permute-start(f32[5,24,128]{2,1,0:T(8,128)S(1)} %get-tuple-element.19.right_ref), channel_id=1, source_target_pairs={{0,1},{1,2},{2,3},{3,4},{4,5},{5,6},{6,7},{7,0},{8,9},{9,10},{10,1... | collective-permute-start | bytes 184328 | tf_op jit(solution)/shard_map/ppermute | solution.py:327

commit v5 on v4

v5 whole, which is shorter than its diff:
```python
import jax
import jax.numpy as jnp
from jax import lax
from jax.experimental import pallas as pl
from jax.experimental.pallas import tpu as pltpu
from jax.sharding import PartitionSpec as P

ITERS = 3
pull_rate = 1.0
smooth_rate = 0.16

NZ = 32
BY = 16
HY = 8
RY = BY + HY
LX = 128
EX = LX // NZ
ZG = 8
GROUPS = NZ // ZG

VMEM = pltpu.VMEM
f32 = jnp.float32
vmem = pl.BlockSpec(memory_space=VMEM)
smem = pl.BlockSpec(memory_space=pltpu.SMEM)


def params(mib):
    return pltpu.CompilerParams(vmem_limit_bytes=mib * 2**20)


def iota(shape, dim):
    return lax.broadcasted_iota(jnp.int32, shape, dim)


def cut_kernel(slab_ref, out_ref):
    count = slab_ref.shape[0]
    low = iota((HY, LX), 0) < HY // 2
    zero = jnp.zeros((HY, LX), f32)
    for i in range(count):
        after = slab_ref[i + 1, 0:HY] if i + 1 < count else zero
        before = slab_ref[i - 1, HY:BY] if i else zero
        out_ref[i, 0:BY] = slab_ref[i]
        out_ref[i, BY:RY] = jnp.where(low, after, before)


def cut(slab):
    count = slab.shape[1] // BY
    return pl.pallas_call(
        cut_kernel,
        out_shape=jax.ShapeDtypeStruct((count, RY, LX), f32),
        in_specs=[vmem],
        out_specs=vmem,
        compiler_params=params(4),
        name="cut",
    )(slab.reshape(count, BY, LX))


def chain_neighbours(chain):
    lane = iota((RY, LX), 1)
    j = lane % EX
    first, last = j == 0, j == EX - 1
    low, high = lane < EX, lane >= LX - EX
    above = [pltpu.roll(p, LX - EX, 1) for p in chain]
    below = [pltpu.roll(p, EX, 1) for p in chain]
    out = []
    for k, p in enumerate(chain):
        before = jnp.where(last, above[k - 1], p) if k else p
        after = jnp.where(first, below[k + 1], p) if k + 1 < len(chain) else p
        out.append(
            (
                jnp.where(high, 0.0, above[k]),
                jnp.where(low, 0.0, below[k]),
                pltpu.roll(p, RY - 1, 0),
                pltpu.roll(p, 1, 0),
                pltpu.roll(after, LX - 1, 1),
                pltpu.roll(before, 1, 1),
            )
        )
    return out


def total(neighbours):
    above, below, after_y, before_y, after_x, before_x = neighbours
    return ((above + below) + (after_y + before_y)) + (after_x + before_x)


def ring(core, after, before):
    return jnp.concatenate([core, after, before], axis=0)


def pack_rows(rows, refs, which):
    group = iota((RY, LX), 1) // EX
    packs = [jnp.zeros((RY, LX), f32)] * 4
    offsets = (1, 2, 0, -1)
    for z in range(NZ):
        turned = pltpu.roll(rows(z), (EX * (z + 1)) % LX, 1)
        packs = [jnp.where(group == (z + at) % NZ, turned, p) for at, p in zip(offsets, packs)]
    for at, p, ref in zip(offsets, packs, refs):
        ref[which] = pltpu.roll(p, (-EX * at) % LX, 1) if at else p


def tissue_rows(tissue_ref, column, group):
    row = iota((RY, LX), 0)

    def at(k):
        return tissue_ref[(group * 3 + k) * 3 + column]

    return jnp.where(row < BY, at(1), jnp.where(row < BY + HY // 2, at(2), at(0)))


def prepare_kernel(
    tissue_ref,
    inside_ref,
    fixed_ref,
    field_ref,
    after_ref,
    before_ref,
    left_ref,
    left_in_ref,
    right_ref,
    right_in_ref,
    cell_ref,
    keep_ref,
    edge_cell_ref,
    edge_keep_ref,
    edge_inside_ref,
):
    zero = jnp.zeros((RY, LX), f32)
    lane = iota((RY, LX), 1)
    cells = [tissue_rows(tissue_ref, 1, g) for g in range(GROUPS)]
    for g in range(GROUPS):
        own = cells[g]
        cell_ref[g] = own
        spread = smooth_rate * own
        flat = 2.0 * own + pltpu.roll(own, 1, 0) + pltpu.roll(own, RY - 1, 0)
        below = cells[g - 1] if g else zero
        above = cells[g + 1] if g + 1 < GROUPS else zero
        keep_ref[3 * g] = 1.0 - spread * (flat + below + own)
        keep_ref[3 * g + 1] = 1.0 - spread * (flat + own + own)
        keep_ref[3 * g + 2] = 1.0 - spread * (flat + own + above)
    for side, columns in enumerate(((0, 1, 1), (1, 1, 2))):
        edge_inside_ref[side] = jnp.full((RY, LX), inside_ref[side], f32)
        chain = []
        for column in columns:
            cell = tissue_rows(tissue_ref, column, GROUPS - 1)
            for g in range(GROUPS - 2, -1, -1):
                cell = jnp.where(lane < (g + 1) * ZG * EX, tissue_rows(tissue_ref, column, g), cell)
            chain.append(cell)
        for k, (t, near) in enumerate(zip(chain, chain_neighbours(chain))):
            edge_cell_ref[side, k] = t
            edge_keep_ref[side, k] = 1.0 - smooth_rate * t * total(near)
    for which in range(4):

        def rows(z):
            x = fixed_ref[z] if which == 3 else field_ref[which, z]
            x = ring(x, after_ref[which, z], before_ref[which, z])
            return x if which == 3 else cells[z // ZG] * x

        pack_rows(rows, (left_ref, left_in_ref, right_ref, right_in_ref), which)


def pack_moving_kernel(moving_ref, *refs):
    pack_rows(lambda z: moving_ref[z], refs[-4:], 4)


PACK = jax.ShapeDtypeStruct((5, RY, LX), f32)


def prepare(tissue, inside, fixed, field, after, before):
    def shape(*dims):
        return jax.ShapeDtypeStruct(dims + (RY, LX), f32)

    return pl.pallas_call(
        prepare_kernel,
        out_shape=(PACK,) * 4 + (shape(GROUPS), shape(3 * GROUPS), shape(2, 3), shape(2, 3), shape(2)),
        in_specs=[smem, smem] + [vmem] * 4,
        out_specs=(vmem,) * 9,
        compiler_params=params(8),
        cost_estimate=pl.CostEstimate(flops=20000000000, bytes_accessed=2**20, transcendentals=0),
        name="prepare",
    )(tissue, inside, fixed, field, after, before)


def pack_moving(moving, *packs):
    return pl.pallas_call(
        pack_moving_kernel,
        out_shape=(PACK,) * 4,
        in_specs=[vmem] * 5,
        out_specs=(vmem,) * 4,
        input_output_aliases={1: 0, 2: 1, 3: 2, 4: 3},
        compiler_params=params(4),
        name="pack_moving",
    )(moving, *packs)


def recip(x):
    r = pl.reciprocal(x, approx=True)
    return r * (2.0 - x * r)


def energy_of(s):
    return s[0] * s[0] + s[1] * s[1] + s[2] * s[2] + 0.5


def attract(field, slopes, gap, energy, tissue):
    residual = gap - (slopes[0] * field[0] + slopes[1] * field[1] + slopes[2] * field[2])
    rate = pull_rate * tissue * residual * recip(energy + residual * residual)
    return [field[c] + rate * slopes[c] for c in range(3)]


def core_kernel(
    moving_ref,
    fixed_ref,
    field_ref,
    after_ref,
    before_ref,
    cell_ref,
    keep_ref,
    out_ref,
    slope_ref,
    energy_ref,
    gap_ref,
    ping_ref,
    pong_ref,
):
    top, end = HY, HY + RY
    zero = jnp.zeros((RY, LX), f32)
    for ref in (ping_ref, pong_ref):
        for c in range(3):
            ref[c, 0, top:end] = zero
            ref[c, NZ + 1, top:end] = zero

    def put(ref, z, pulled):
        for c in range(3):
            ref[c, z + 1, top:end] = pulled[c]
            ref[c, z + 1, 0:top] = pulled[c][BY:]
            ref[c, z + 1, end : end + HY] = pulled[c][:HY]

    for z in range(NZ):
        m = moving_ref[z]
        above = moving_ref[z + 1] if z < NZ - 1 else zero
        below = moving_ref[z - 1] if z else zero
        s = [
            0.5 * (above - below),
            0.5 * (pltpu.roll(m, RY - 1, 0) - pltpu.roll(m, 1, 0)),
            0.5 * (pltpu.roll(m, LX - 1, 1) - pltpu.roll(m, 1, 1)),
        ]
        energy = energy_of(s)
        gap = ring(fixed_ref[z], after_ref[3, z], before_ref[3, z]) - m
        t = cell_ref[z // ZG]
        field = [t * ring(field_ref[c, z], after_ref[c, z], before_ref[c, z]) for c in range(3)]
        put(ping_ref, z, attract(field, s, gap, energy, t))
        for c in range(3):
            slope_ref[c, z] = s[c]
        energy_ref[z] = energy
        gap_ref[z] = gap

    def smoothed(src, z, c, rows):
        def at(dz, dy):
            return src[c, z + 1 + dz, top + dy : top + dy + rows]

        p = at(0, 0)
        around = (
            (at(1, 0) + at(-1, 0)) + (at(0, 1) + at(0, -1)) + (pltpu.roll(p, 1, 1) + pltpu.roll(p, LX - 1, 1))
        )
        g, k = z // ZG, z % ZG
        keep = keep_ref[3 * g + (0 if k == 0 else 2 if k == ZG - 1 else 1), 0:rows]
        return keep * p + (smooth_rate * cell_ref[g, 0:rows]) * around

    src, dst = ping_ref, pong_ref
    for sweep in range(ITERS - 1):
        for z in range(NZ):
            field = [smoothed(src, z, c, RY) for c in range(3)]
            s = [slope_ref[c, z] for c in range(3)]
            put(dst, z, attract(field, s, gap_ref[z], energy_ref[z], cell_ref[z // ZG]))
        src, dst = dst, src
    for z in range(NZ):
        for c in range(3):
            out_ref[c, z] = smoothed(src, z, c, BY)


def core(moving, fixed, field, after, before, cell, keep):
    return pl.pallas_call(
        core_kernel,
        out_shape=jax.ShapeDtypeStruct((3, NZ, BY, LX), f32),
        in_specs=[vmem] * 7,
        out_specs=vmem,
        scratch_shapes=[
            VMEM((3, NZ, RY, LX), f32),
            VMEM((NZ, RY, LX), f32),
            VMEM((NZ, RY, LX), f32),
            VMEM((3, NZ + 2, RY + 2 * HY, LX), f32),
            VMEM((3, NZ + 2, RY + 2 * HY, LX), f32),
        ],
        compiler_params=params(16),
        cost_estimate=pl.CostEstimate(flops=10000000000, bytes_accessed=2**20, transcendentals=0),
        name="core",
    )(moving, fixed, field, after, before, cell, keep)


def edge_kernel(
    left_ref,
    left_in_ref,
    right_ref,
    right_in_ref,
    got_left_ref,
    got_right_ref,
    cell_ref,
    keep_ref,
    inside_ref,
    core_ref,
    out_ref,
):
    lane = iota((RY, LX), 1)
    chains = ((got_left_ref, left_ref, left_in_ref), (right_in_ref, right_ref, got_right_ref))
    moving = [
        [chains[0][0][4] * inside_ref[0], chains[0][1][4], chains[0][2][4]],
        [chains[1][0][4], chains[1][1][4], chains[1][2][4] * inside_ref[1]],
    ]
    tissue = [[cell_ref[e, k] for k in range(3)] for e in range(2)]
    slopes = [
        [[0.5 * (n[0] - n[1]), 0.5 * (n[2] - n[3]), 0.5 * (n[4] - n[5])] for n in chain_neighbours(m)] for m in moving
    ]
    energy = [[energy_of(x) for x in s] for s in slopes]
    gap = [[ref[3] - x for ref, x in zip(refs, m)] for refs, m in zip(chains, moving)]
    field = [[[t * ref[c] for c in range(3)] for t, ref in zip(ts, refs)] for ts, refs in zip(tissue, chains)]
    for sweep in range(ITERS):
        pulled = [
            [attract(*x) for x in zip(field[e], slopes[e], gap[e], energy[e], tissue[e])] for e in range(2)
        ]
        near = [[chain_neighbours([p[c] for p in pulled[e]]) for c in range(3)] for e in range(2)]
        field = [
            [
                [keep_ref[e, k] * pulled[e][k][c] + smooth_rate * tissue[e][k] * total(near[e][c][k]) for c in range(3)]
                for k in range(3)
            ]
            for e in range(2)
        ]
    left, right = field[0][1], field[1][1]
    even = (lane // EX)[:BY] % 2 == 0
    outer = (lane[:BY] < EX) | (lane[:BY] >= LX - EX)
    both = [[], []]
    for c in range(3):
        a, b = left[c][:BY], right[c][:BY]
        both[0].append(jnp.where(even, b, pltpu.roll(a, EX, 1)))
        both[1].append(jnp.where(even, pltpu.roll(b, LX - EX, 1), a))
    for z in range(NZ):
        for c in range(3):
            turned = pltpu.roll(both[z % 2][c], (-EX * (z // 2 * 2 + 1)) % LX, 1)
            out_ref[c, z] = jnp.where(outer, turned, core_ref[c, z])


def edge(packs, got_left, got_right, weights, middle):
    return pl.pallas_call(
        edge_kernel,
        out_shape=jax.ShapeDtypeStruct((3, NZ, BY, LX), f32),
        in_specs=[vmem] * 10,
        out_specs=vmem,
        compiler_params=params(16),
        name="edge",
    )(*packs, got_left, got_right, *weights, middle)


def turn(x, axis, by):
    size = lax.axis_size(axis)
    return lax.ppermute(x, axis, [(i, (i + by) % size) for i in range(size)])


def body(moving_slab, fixed_image, start_field, tissue_mask):
    row = lax.axis_index("row")
    col = lax.axis_index("col")
    blocks = cut(moving_slab)
    moving = lax.all_to_all(blocks, "row", split_axis=0, concat_axis=0, tiled=True)

    state = jnp.concatenate([start_field, fixed_image[None]], axis=0)
    after = turn(state[:, :, 0 : HY // 2], "row", -1)
    before = turn(state[:, :, BY - HY // 2 :], "row", 1)

    padded = jnp.pad(tissue_mask, ((0, 0), (1, 1), (1, 1))).astype(f32)
    tissue = lax.dynamic_slice(padded, (0, row, col), (GROUPS, 3, 3)).reshape(-1)
    inside = jnp.stack([col > 0, col < lax.axis_size("col") - 1]).astype(f32)

    prepared = prepare(tissue, inside, fixed_image, start_field, after, before)
    cell, keep, *weights = prepared[4:]
    packs = pack_moving(moving, *prepared[:4])
    left, _, right, _ = packs
    got_left = turn(right, "col", 1)
    got_right = turn(left, "col", -1)
    middle = core(moving, fixed_image, start_field, after, before, cell, keep)
    return edge(packs, got_left, got_right, weights, middle)


def solution(mesh):
    in_specs = (P("row", None, "col"), P(None, "row", "col"), P(None, None, "row", "col"), P())
    out_specs = P(None, None, "row", "col")
    return jax.shard_map(body, mesh=mesh, in_specs=in_specs, out_specs=out_specs, check_vma=False)
```

time: 41.2 us -> 39.7 us (0.964)
  Pallas kernels: 8.38 us -> 7.59 us
  waiting for transfers between devices: 11.1 us -> 10.4 us
    pallas_call x1, Pallas kernels: 3.58 us -> 2.59 us  [edge(): pl.pallas_call(edge_kernel, out_shape=jax.ShapeDtypeStruct((3, NZ, BY, LX...]
    pallas_call x2, Pallas kernels: 1.11 us -> 1.77 us  [the longest x1 1.53 us: prepare(): pl.pallas_call(prepare_kernel, out_shape=(PACK,) * 4 + (shape(GROUPS), sh...]
    all_to_all x1, waiting for transfers between devices: 11.1 us -> 10.4 us  [body(): lax.all_to_all(blocks, 'row', split_axis=0, concat_axis=0, tiled=True)]
    pallas_call x1, Pallas kernels: 2.93 us -> 2.47 us  [core(): pl.pallas_call(core_kernel, out_shape=jax.ShapeDtypeStruct((3, NZ, BY, LX...]
  transfers between devices with their start and end apart: 5 -> 5, of which waited for: 1 -> 1; matrix products, arithmetic and copies ran while one was open for 1% -> 1% of each run, Pallas kernels for 11% -> 12%
where the time goes in v5:
time: 39.7 us; the launch traced here: 39.4 us
  starting transfers between devices  18.9 us (48%)
  waiting for transfers between devices  10.4 us (26%)
  Pallas kernels  7.59 us (19%)
  other arithmetic  1.54 us (4%)
  local copies, waits for them, and re-layouts  0.92 us (2%)
    ppermute x4, starting transfers between devices, turn(): return lax.ppermute(x, axis, [(i, (i + by) % size) for i in range(size)])  13.2 us
    all_to_all x1, waiting for transfers between devices, body(): lax.all_to_all(blocks, 'row', split_axis=0, concat_axis=0, tiled=True)  10.4 us
    all_to_all x1, starting transfers between devices, body(): lax.all_to_all(blocks, 'row', split_axis=0, concat_axis=0, tiled=True)  5.63 us
    pallas_call x1, Pallas kernels, edge(): pl.pallas_call(edge_kernel, out_shape=jax.ShapeDtypeStruct((3, NZ, BY, LX...  2.59 us
    pallas_call x1, Pallas kernels, core(): pl.pallas_call(core_kernel, out_shape=jax.ShapeDtypeStruct((3, NZ, BY, LX...  2.47 us
    pallas_call x1, Pallas kernels, prepare(): pl.pallas_call(prepare_kernel, out_shape=(PACK,) * 4 + (shape(GROUPS), sh...  1.53 us
    concatenate x1, other arithmetic, body(): state = jnp.concatenate([start_field, fixed_image[None]], axis=0)  1.38 us
  transfers between devices with their start and end apart: 5, of which 1 were waited for; matrix products, arithmetic and copies ran while one was open for 1% of the time, Pallas kernels for 12%

profile of v5, /device:TPU:1, one launch (start us, length us, event | category | flops | bytes accessed | tf_op | source)
XLA Modules:
  0.0 39.4 jit_solution(11569278555201580909)
XLA Ops:
  0.0 0.0 copy-start.1
  0.0 1.4 %pad_maximum_fusion = (f32[4,32,4,128]{3,2,1,0:T(4,128)S(1)}, f32[4,32,4,128]{3,2,1,0:T(4,128)S(1)}) fusion(f32[1,32,16,128]{3,2,1,0:T(8,128)} %bitcast.5, f32[3,32,16,128]{3,2,1,0:T(8,128)} %field_ref.3), kind=kLoop, calls=%fused_computation | loop fusion | flops 131072 | bytes 1572864 | tf_op jit(solution)/shard_map/concatenate | solution.py:375
  1.4 0.0 copy-start
  1.4 2.1 %collective-permute-start.1 = (f32[4,32,4,128]{3,2,1,0:T(4,128)S(1)}, f32[4,32,4,128]{3,2,1,0:T(4,128)S(1)}, u32[]{:S(2)}, u32[]{:S(2)}) collective-permute-start(f32[4,32,4,128]{3,2,1,0:T(4,128)S(1)} %get-tuple-element.31), channel_id=1, source_target_pairs={{0,8},{8,16},{16,24},{24,32},{32,40},{40,48},{48,56},{56,64},{64,7... | collective-permute-start | bytes 786440 | tf_op jit(solution)/shard_map/ppermute | solution.py:366
  3.5 6.6 %collective-permute-start = (f32[4,32,4,128]{3,2,1,0:T(4,128)S(1)}, f32[4,32,4,128]{3,2,1,0:T(4,128)S(1)}, u32[]{:S(2)}, u32[]{:S(2)}) collective-permute-start(f32[4,32,4,128]{3,2,1,0:T(4,128)S(1)} %get-tuple-element.32), channel_id=1, source_target_pairs={{0,248},{8,0},{16,8},{24,16},{32,24},{40,32},{48,40},{56,48},{64,5... | collective-permute-start | bytes 786440 | tf_op jit(solution)/shard_map/ppermute | solution.py:366
  10.2 0.0 copy-done.1
  10.2 0.8 %cut.1 = f32[32,24,128]{2,1,0:T(8,128)} custom-call(f32[32,16,128]{2,1,0:T(8,128)S(1)} %bitcast.4), custom_call_target="tpu_custom_call" | custom-call | tf_op jit(solution)/shard_map/cut/pallas_call | solution.py:48
  10.9 0.0 copy-start.2
  10.9 5.6 %all-to-all-start = ((f32[32,24,128]{2,1,0:T(8,128)}), f32[32,24,128]{2,1,0:T(8,128)S(1)}, u32[]{:S(2)}, u32[]{:S(2)}) async-start(f32[32,24,128]{2,1,0:T(8,128)} %cut.1), calls=%async_computation | async-start | bytes 786432 | tf_op jit(solution)/shard_map/all_to_all | solution.py:373
  16.6 0.0 copy-start.3
  16.6 0.7 %copy-done.3 = s32[4,32,8]{1,2,0:T(8,128)S(1)} copy-done((s32[4,32,8]{1,2,0:T(8,128)S(1)}, s32[4,32,8]{1,2,0:T(8,128)}, u32[]{:S(2)}) %copy-start.3) | copy-done | bytes 4120
  17.3 0.1 fusion
  17.4 0.1 copy.10
  17.5 0.1 reshape.7.tissue_ref
  17.6 0.1 add_convert_fusion.inside_ref
  17.7 0.0 collective-permute-done.1.before_ref
  17.7 0.0 collective-permute-done.after_ref
  17.7 0.0 copy-done
  17.7 0.0 copy-done.2
  17.7 1.5 %prepare.1 = (f32[5,24,128]{2,1,0:T(8,128)S(1)}, f32[5,24,128]{2,1,0:T(8,128)S(1)}, f32[5,24,128]{2,1,0:T(8,128)S(1)}, f32[5,24,128]{2,1,0:T(8,128)S(1)}, f32[4,...) custom-call(f32[36]{0:T(128)S(1)} %reshape.7.tissue_ref, ...), custom_call_target="tpu_custom_call" | custom-call | flops 20000000000 | bytes 1048576 | tf_op jit(solution)/shard_map/prepare/pallas_call | solution.py:173
  19.2 10.4 %all-to-all-done.moving_ref = f32[32,24,128]{2,1,0:T(8,128)S(1)} async-done(((f32[32,24,128]{2,1,0:T(8,128)}), f32[32,24,128]{2,1,0:T(8,128)S(1)}, u32[]{:S(2)}, u32[]{:S(2)}) %all-to-all-start) | async-done | bytes 393248 | tf_op jit(solution)/shard_map/all_to_all | solution.py:373
  29.6 0.2 pack_moving.1
  29.9 3.3 %collective-permute-start.3 = (f32[5,24,128]{2,1,0:T(8,128)S(1)}, f32[5,24,128]{2,1,0:T(8,128)S(1)}, u32[]{:S(2)}, u32[]{:S(2)}) collective-permute-start(f32[5,24,128]{2,1,0:T(8,128)S(1)} %get-tuple-element.22.left_ref), channel_id=1, source_target_pairs={{0,7},{1,0},{2,1},{3,2},{4,3},{5,4},{6,5},{7,6},{8,15},{9,8},{10,9... | collective-permute-start | bytes 184328 | tf_op jit(solution)/shard_map/ppermute | solution.py:366
  33.1 1.2 %collective-permute-start.2 = (f32[5,24,128]{2,1,0:T(8,128)S(1)}, f32[5,24,128]{2,1,0:T(8,128)S(1)}, u32[]{:S(2)}, u32[]{:S(2)}) collective-permute-start(f32[5,24,128]{2,1,0:T(8,128)S(1)} %get-tuple-element.24.right_ref), channel_id=1, source_target_pairs={{0,1},{1,2},{2,3},{3,4},{4,5},{5,6},{6,7},{7,0},{8,9},{9,10},{10,1... | collective-permute-start | bytes 184328 | tf_op jit(solution)/shard_map/ppermute | solution.py:366
  34.3 2.5 %core.1.core_ref = f32[3,32,16,128]{3,2,1,0:T(8,128)S(1)} custom-call(f32[32,24,128]{2,1,0:T(8,128)S(1)} %all-to-all-done.moving_ref, f32[32,16,128]{2,1,0:T(8,128)S(1)} %copy-done.2, f32[3,32,16,128]{3,2,1,0:T(8,128)S(1)} %copy-done, f32[4,32,4,128]{3,2,1,0:T(4,128)S(1)} %collective-permute-done.after_ref, ...), custom_call_target="tpu_custom_call" | custom-call | flops 10000000000 | bytes 1048576 | tf_op jit(solution)/shard_map/core/pallas_call | solution.py:283
  36.8 0.0 collective-permute-done.3.got_right_ref
  36.8 0.0 collective-permute-done.2.got_left_ref
  36.8 2.6 %edge.1 = f32[3,32,16,128]{3,2,1,0:T(8,128)} custom-call(f32[5,24,128]{2,1,0:T(8,128)S(1)} %get-tuple-element.22.left_ref, f32[5,24,128]{2,1,0:T(8,128)S(1)} %get-tuple-element.23.left_in_ref, f32[5,24,128]{2,1,0:T(8,128)S(1)} %get-tuple-element.24.right_ref, f32[5,24,128]{2,1,0:T(8,128)S(1)} %get-tuple-element.25.right_in_ref, ...), custom_call_target="tpu_custom_call" | custom-call | tf_op jit(solution)/shard_map/edge/pallas_call | solution.py:354
Async XLA Ops:
  0.0 10.2 %copy-start.1 = (f32[1,512,128]{2,1,0:T(8,128)S(1)}, f32[1,512,128]{2,1,0:T(8,128)}, u32[]{:S(2)}) copy-start(f32[1,512,128]{2,1,0:T(8,128)} %param.4) | copy-start | bytes 786436
  1.4 16.3 %copy-start = (f32[3,32,16,128]{3,2,1,0:T(8,128)S(1)}, f32[3,32,16,128]{3,2,1,0:T(8,128)}, u32[]{:S(2)}) copy-start(f32[3,32,16,128]{3,2,1,0:T(8,128)} %field_ref.3) | copy-start | bytes 2359300
  1.4 16.3 %collective-permute-start.1 = (f32[4,32,4,128]{3,2,1,0:T(4,128)S(1)}, f32[4,32,4,128]{3,2,1,0:T(4,128)S(1)}, u32[]{:S(2)}, u32[]{:S(2)}) collective-permute-start(f32[4,32,4,128]{3,2,1,0:T(4,128)S(1)} %get-tuple-element.31), channel_id=1, source_target_pairs={{0,8},{8,16},{16,24},{24,32},{32,40},{40,48},{48,56},{56,64},{64,7... | collective-permute-start | bytes 786440 | tf_op jit(solution)/shard_map/ppermute | solution.py:366
  3.5 14.2 %collective-permute-start = (f32[4,32,4,128]{3,2,1,0:T(4,128)S(1)}, f32[4,32,4,128]{3,2,1,0:T(4,128)S(1)}, u32[]{:S(2)}, u32[]{:S(2)}) collective-permute-start(f32[4,32,4,128]{3,2,1,0:T(4,128)S(1)} %get-tuple-element.32), channel_id=1, source_target_pairs={{0,248},{8,0},{16,8},{24,16},{32,24},{40,32},{48,40},{56,48},{64,5... | collective-permute-start | bytes 786440 | tf_op jit(solution)/shard_map/ppermute | solution.py:366
  10.9 6.7 %copy-start.2 = (f32[32,16,128]{2,1,0:T(8,128)S(1)}, f32[32,16,128]{2,1,0:T(8,128)}, u32[]{:S(2)}) copy-start(f32[32,16,128]{2,1,0:T(8,128)} %fixed_ref.3) | copy-start | bytes 786436
  10.9 18.7 %all-to-all-start = ((f32[32,24,128]{2,1,0:T(8,128)}), f32[32,24,128]{2,1,0:T(8,128)S(1)}, u32[]{:S(2)}, u32[]{:S(2)}) async-start(f32[32,24,128]{2,1,0:T(8,128)} %cut.1), calls=%async_computation | async-start | bytes 786432 | tf_op jit(solution)/shard_map/all_to_all | solution.py:373
  16.6 0.7 %copy-start.3 = (s32[4,32,8]{1,2,0:T(8,128)S(1)}, s32[4,32,8]{1,2,0:T(8,128)}, u32[]{:S(2)}) copy-start(s32[4,32,8]{1,2,0:T(8,128)} %param.7) | copy-start | bytes 12292
  29.9 7.0 %collective-permute-start.3 = (f32[5,24,128]{2,1,0:T(8,128)S(1)}, f32[5,24,128]{2,1,0:T(8,128)S(1)}, u32[]{:S(2)}, u32[]{:S(2)}) collective-permute-start(f32[5,24,128]{2,1,0:T(8,128)S(1)} %get-tuple-element.22.left_ref), channel_id=1, source_target_pairs={{0,7},{1,0},{2,1},{3,2},{4,3},{5,4},{6,5},{7,6},{8,15},{9,8},{10,9... | collective-permute-start | bytes 184328 | tf_op jit(solution)/shard_map/ppermute | solution.py:366
  33.1 3.7 %collective-permute-start.2 = (f32[5,24,128]{2,1,0:T(8,128)S(1)}, f32[5,24,128]{2,1,0:T(8,128)S(1)}, u32[]{:S(2)}, u32[]{:S(2)}) collective-permute-start(f32[5,24,128]{2,1,0:T(8,128)S(1)} %get-tuple-element.24.right_ref), channel_id=1, source_target_pairs={{0,1},{1,2},{2,3},{3,4},{4,5},{5,6},{6,7},{7,0},{8,9},{9,10},{10,1... | collective-permute-start | bytes 184328 | tf_op jit(solution)/shard_map/ppermute | solution.py:366
